TPU v7x, 32 devices: a whole 2x2x4 slice. The times are simulated.
32 devices in a mesh: plane: 8 (over z, x), depth: 4 (over y, core).
Axes of the slice: x: 2, y: 2, z: 4, core: 2. Of those that a mesh axis runs over, the one named last changes fastest.
Arguments:
- density: float32 [64, 32768], P(None, ('plane', 'depth')), may hold values from 0.01 to 1
- energy: float32 [64, 32768], P(None, ('plane', 'depth')), may hold values from 0.1 to 10
- links: int32 [27, 32768], P(None, ('plane', 'depth')), may hold values from 0 to 3584, as said below
- send_index: int32 [8, 4, 4, 512], P('plane', 'depth'), may hold values from 0 to 1023
- send_live: int32 [8, 4, 4], P('plane', 'depth'), may hold values from 128 to 512, as said below
- face_index: int32 [8, 4, 2, 256], P('plane', 'depth'), may hold values from 0 to 1023
Outputs:
- conductivity: float32 [64, 32768], P(None, ('plane', 'depth'))
- sensitivity: float32 [64, 32768], P(None, ('plane', 'depth'))
Inputs may be any that keep to these rules, and one draw needn't show every extreme that they name: `links`: the slot 13 of every block names the block itself; column 3584 stands for a neighbour outside the design domain. `send_live`: every brick has one plane neighbour whose list is full.
All inputs are finite; a program needn't handle non-finite values.
Results may differ from a plain program's by a relative error of at most 0.0003.
Values sent between devices are 32-bit elements; how exact they have to be, the bound alone decides.
A program may use at most 64 MiB of HBM per device.

v0:
```python
import jax
import jax.numpy as jnp
from jax import lax
from jax.sharding import PartitionSpec as P

REACH = 2


radius = 3.0
floor_value = 0.001
penalty = 3.0


def passed_along(shard, axis, by):
    count = lax.axis_size(axis)
    pairs = [(i, i + by) for i in range(count) if 0 <= i + by < count]
    return lax.ppermute(shard, axis, pairs)


def padded(shard, sides, width):
    for axis, dim in sides:
        count, length = (lax.axis_size(axis), shard.shape[dim])
        up = [(i, (i + 1) % count) for i in range(count - 1)]
        down = [(j, i) for i, j in up]
        last = lax.slice_in_dim(shard, length - width, length, axis=dim)
        first = lax.slice_in_dim(shard, 0, width, axis=dim)
        before = lax.ppermute(last, axis, up)
        after = lax.ppermute(first, axis, down)
        shard = jnp.concatenate([before, shard, after], axis=dim)
    return shard


def cone_table():
    voxels = jnp.arange(64)
    places = jnp.stack([voxels // 16, voxels // 4 % 4, voxels % 4], axis=-1).astype(jnp.float32)
    slots = jnp.arange(27)
    moved = (
        jnp.stack([slots // 9 - 1, slots // 3 % 3 - 1, slots % 3 - 1], axis=-1).astype(jnp.float32)
        * 4.0
    )
    apart = places[None, :, None, :] - places[None, None, :, :] - moved[:, None, None, :]
    return jnp.maximum(0.0, radius - jnp.sqrt(jnp.sum(apart * apart, axis=-1)))


def local_rows(ext_rows, link_table, energy_rows, table):
    width = ext_rows.shape[0]
    row_sums = jnp.sum(table, axis=2)
    valid = (link_table != width - 1).astype(jnp.float32)
    weight_sum = jnp.dot(valid.T, row_sums, precision=lax.Precision.HIGHEST)
    picked = jnp.take(ext_rows, link_table, axis=0)
    filtered = jnp.einsum("kbj,kij->bi", picked, table, precision=lax.Precision.HIGHEST)
    filtered = filtered / weight_sum
    conductivity = floor_value + filtered * filtered * filtered * (1.0 - floor_value)
    scaled = -penalty * (1.0 - floor_value) * filtered * filtered * energy_rows / weight_sum
    spread = jnp.einsum("bi,kij->kbj", scaled, table, precision=lax.Precision.HIGHEST)
    back = (
        jnp.zeros((width, 64), jnp.float32).at[link_table.reshape(-1)].add(spread.reshape(-1, 64))
    )
    return (conductivity, back)


def on_device(density, energy, links, send_index, send_live, face_index):
    table = cone_table()
    blocks = density.shape[1]
    dens_rows = density.T
    energy_rows = energy.T
    indices = send_index[0, 0]
    counts = send_live[0, 0]
    faces_at = face_index[0, 0]
    capacity = indices.shape[1]
    keep = (jnp.arange(capacity)[None, :] < counts[:, None]).astype(jnp.float32)
    payload = jnp.take(dens_rows, indices, axis=0) * keep[:, :, None]
    offsets = [offset for offset in range(-REACH, REACH + 1) if offset != 0]
    received = [
        passed_along(payload[member], "plane", offset) for member, offset in enumerate(offsets)
    ]
    face_load = jnp.take(dens_rows, faces_at, axis=0)
    rims = padded(face_load, (("depth", 0),), 1)
    ext_rows = jnp.concatenate(
        [dens_rows] + received + [rims[0], rims[3], jnp.zeros((1, 64), jnp.float32)], axis=0
    )
    conductivity, back = local_rows(ext_rows, links, energy_rows, table)
    sens = back[:blocks]
    groups_back = [
        back[blocks + member * capacity : blocks + (member + 1) * capacity]
        for member in range(len(offsets))
    ]
    returned = [
        passed_along(groups_back[member], "plane", -offset) for member, offset in enumerate(offsets)
    ]
    low_start = blocks + len(offsets) * capacity
    face_count = faces_at.shape[1]
    face_back = jnp.stack(
        [
            back[low_start : low_start + face_count],
            back[low_start + face_count : low_start + 2 * face_count],
        ]
    )
    rims_back = padded(face_back, (("depth", 0),), 1)
    values = [returned[member] * keep[member][:, None] for member in range(len(offsets))] + [
        rims_back[0],
        rims_back[3],
    ]
    places = [indices[member] for member in range(len(offsets))] + [faces_at[0], faces_at[1]]
    sens = sens.at[jnp.concatenate(places)].add(jnp.concatenate(values, axis=0))
    return (conductivity.T, sens.T)


def solution(mesh):
    in_specs = (
        P(None, ("plane", "depth")),
        P(None, ("plane", "depth")),
        P(None, ("plane", "depth")),
        P("plane", "depth", None, None),
        P("plane", "depth", None),
        P("plane", "depth", None, None),
    )
    out_specs = (P(None, ("plane", "depth")), P(None, ("plane", "depth")))
    return jax.shard_map(
        on_device, mesh=mesh, in_specs=in_specs, out_specs=out_specs, check_vma=False
    )
```

profile of v0, /device:TPU:0, one launch (start us, length us, event | category | flops | bytes accessed | tf_op | source)
XLA Modules:
  0.0 354.1 jit_solution(1027278499830497701)
XLA Ops:
  0.6 1.1 copy.26
  1.8 0.7 fusion.29
  2.5 0.8 fusion.30
  3.3 5.5 %gather_fusion = f32[2048,64]{1,0:T(8,128)S(1)} fusion(f32[1024,64]{1,0:T(8,128)S(1)} %bitcast.85, s32[2048]{0:T(1024)S(1)} %broadcast_clamp_fusion.1), kind=kCustom, calls=%fused_computation | custom fusion | bytes 1056768 | tf_op jit(solution)/shard_map/jit(_take)/gather | solution.py:72
  8.8 0.7 select_multiply_fusion
  9.5 1.0 slice_bitcast_fusion
  10.5 1.3 collective-permute-start
  11.7 1.3 collective-permute-start.1
  13.0 6.2 %collective-permute-start.2 = (f32[512,64]{1,0:T(8,128)}, f32[512,64]{1,0:T(8,128)}, u32[]{:S(2)}, u32[]{:S(2)}) collective-permute-start(f32[512,64]{1,0:T(8,128)} %get-tuple-element.15), channel_id=1, source_target_pairs={{0,4},{4,8},{8,12},{12,16},{16,20},{20,24},{24,28},{1,5},{5,9},{9,... | collective-permute-start | bytes 393224 | tf_op jit(solution)/shard_map/ppermute | solution.py:17
  19.2 3.9 %collective-permute-start.3 = (f32[512,64]{1,0:T(8,128)}, f32[512,64]{1,0:T(8,128)S(1)}, u32[]{:S(2)}, u32[]{:S(2)}) collective-permute-start(f32[512,64]{1,0:T(8,128)} %get-tuple-element.14), channel_id=1, source_target_pairs={{0,8},{4,12},{8,16},{12,20},{16,24},{20,28},{1,9},{5,13},{9,17},{1... | collective-permute-start | bytes 393224 | tf_op jit(solution)/shard_map/ppermute | solution.py:17
  23.3 1.0 gather_fusion.1
  24.3 0.1 broadcast_select_fusion
  24.5 0.7 fusion.46
  25.2 1.9 collective-permute-start.4
  27.3 0.6 fusion.47
  28.0 0.1 broadcast_subtract_fusion
  28.1 0.1 copy.28
  28.2 0.5 multiply_reduce_fusion
  28.6 0.4 fusion.12
  29.0 0.3 fusion.25
  29.4 0.1 copy.38
  29.5 0.8 compare_select_fusion
  30.4 1.3 collective-permute-start.5
  31.7 1.0 constant_dynamic-update-slice_fusion.3
  32.6 1.0 constant_dynamic-update-slice_fusion.2
  33.6 1.0 constant_dynamic-update-slice_fusion.1
  34.7 0.9 bitcast_dynamic-update-slice_fusion.3
  35.6 91.5 %gather_fusion.2 = f32[27648,64]{1,0:T(8,128)} fusion(f32[3585,64]{1,0:T(8,128)S(1)} %dynamic-update-slice.19, s32[27648]{0:T(1024)S(1)} %broadcast_clamp_fusion), kind=kCustom, calls=%fused_computation.2 | custom fusion | bytes 14266368 | tf_op jit(solution)/shard_map/jit(_take)/gather | solution.py:50
  127.1 11.8 %copy.27 = f32[27,1024,64]{1,2,0:T(8,128)} copy(f32[27,1024,64]{2,1,0:T(8,128)} %bitcast.87) | data formatting | bytes 14155776 | tf_op jit(solution)/shard_map/jit(_take)/gather | solution.py:50
  138.9 8.4 %fusion.18 = (f32[64,1024]{1,0:T(8,128)}, f32[1024,64]{0,1:T(8,128)S(1)}) fusion(f32[1024,64]{0,1:T(8,128)S(1)} %fusion.25, f32[27,64,64]{2,1,0:T(8,128)S(1)} %multiply_reduce_fusion, f32[27,1024,64]{1,2,0:T(8,128)} %copy.27, pred[27,1024]{1,0:T(8,128)(4,1)S(1)} %compare_and_fusion), kind=kOutput, calls=%fused_computation.27 | convolution fusion | flops 1361272832 | bytes 8334336 | tf_op jit(solution)/shard_map/kbj,kij->bi/dot_general | solution.py:51
  147.2 7.8 %convolution_bitcast_fusion = f32[27,1024,64]{1,2,0:T(8,128)} fusion(f32[27,64,64]{2,1,0:T(8,128)S(1)} %multiply_reduce_fusion, f32[1024,64]{0,1:T(8,128)S(1)} %fusion.25, f32[1024,64]{0,1:T(8,128)S(1)} %get-tuple-element.25, f32[64,1024]{1,0:T(8,128)S(1)} %copy-done.2), kind=kOutput, calls=%fused_computation.9 | convolution fusion | flops 1359437824 | bytes 8306688 | tf_op jit(solution)/shard_map/bi,kij->kbj/dot_general | solution.py:55
  155.0 10.7 %copy.34 = f32[27,1024,64]{2,1,0:T(8,128)} copy(f32[27,1024,64]{1,2,0:T(8,128)} %convolution_bitcast_fusion) | data formatting | bytes 14155776 | tf_op jit(solution)/shard_map/reshape | solution.py:57
  165.7 147.7 %scatter_custom_fusion = f32[3585,64]{1,0:T(8,128)S(1)} fusion(s32[27648]{0:T(1024)} %bitcast.93, f32[27648,64]{1,0:T(8,128)} %bitcast.88, f32[]{:T(128)} %constant.125.clone.1), kind=kCustom, calls=%fused_computation.14 | custom fusion | flops 1769472 | bytes 918272 | tf_op jit(solution)/shard_map/scatter-add | solution.py:57
  313.4 0.1 fusion.45
  313.5 3.9 %collective-permute-start.6 = (f32[512,64]{1,0:T(8,128)S(1)}, f32[512,64]{1,0:T(8,128)S(1)}, u32[]{:S(2)}, u32[]{:S(2)}) collective-permute-start(f32[512,64]{1,0:T(8,128)S(1)} %get-tuple-element.13), channel_id=1, source_target_pairs={{0,8},{4,12},{8,16},{12,20},{16,24},{20,28},{1,9},{5,13},{9,17},{1... | collective-permute-start | bytes 393224 | tf_op jit(solution)/shard_map/ppermute | solution.py:17
  317.4 4.3 %collective-permute-start.7 = (f32[512,64]{1,0:T(8,128)S(1)}, f32[512,64]{1,0:T(8,128)S(1)}, u32[]{:S(2)}, u32[]{:S(2)}) collective-permute-start(f32[512,64]{1,0:T(8,128)S(1)} %get-tuple-element.12), channel_id=1, source_target_pairs={{0,4},{4,8},{8,12},{12,16},{16,20},{20,24},{24,28},{1,5},{5,9},{9,... | collective-permute-start | bytes 393224 | tf_op jit(solution)/shard_map/ppermute | solution.py:17
  321.8 1.3 collective-permute-start.8
  323.1 1.3 collective-permute-start.9
  324.4 4.2 %collective-permute-start.10 = (f32[1,256,64]{2,1,0:T(8,128)S(1)}, f32[1,256,64]{2,1,0:T(8,128)S(1)}, u32[]{:S(2)}, u32[]{:S(2)}) collective-permute-start(f32[1,256,64]{2,1,0:T(8,128)S(1)} %get-tuple-element.9), channel_id=1, source_target_pairs={{0,1},{1,2},{2,3},{4,5},{5,6},{6,7},{8,9},{9,10},{10,11},{12,13},{... | collective-permute-start | bytes 196616 | tf_op jit(solution)/shard_map/ppermute | solution.py:27
  328.7 1.4 collective-permute-start.11
  330.1 0.1 multiply_dynamic-update-slice_fusion.3
  330.3 0.1 multiply_dynamic-update-slice_fusion.2
  330.4 0.7 collective-permute-done.8
  331.1 0.1 multiply_dynamic-update-slice_fusion.1
  331.3 7.3 %collective-permute-done.9 = f32[512,64]{1,0:T(8,128)S(1)} collective-permute-done((f32[512,64]{1,0:T(8,128)S(1)}, f32[512,64]{1,0:T(8,128)S(1)}, u32[]{:S(2)}, u32[]{:S(2)}) %collective-permute-start.9) | collective-permute-done | bytes 131104 | tf_op jit(solution)/shard_map/ppermute | solution.py:17
  338.6 0.1 multiply_dynamic-update-slice_fusion
  338.8 14.4 %scatter_fusion = f32[1024,64]{1,0:T(8,128)S(1)} fusion(f32[1024,64]{1,0:T(8,128)S(1)} %slice-done, s32[2560]{0:T(1024)S(1)} %fusion.28, f32[2560,64]{1,0:T(8,128)S(1)} %bitcast_dynamic-update-slice_fusion), kind=kCustom, calls=%fused_computation.4 | custom fusion | flops 163840 | bytes 1976320 | tf_op jit(solution)/shard_map/scatter-add | solution.py:105
  353.2 0.9 copy.32
  (57 shorter events, 0.5 us)
Async XLA Ops:
  8.8 14.4 %copy-start.4 = (s32[1,1,2,256]{3,2,1,0:T(2,128)S(1)}, s32[1,1,2,256]{3,2,1,0:T(2,128)}, u32[]{:S(2)}) copy-start(s32[1,1,2,256]{3,2,1,0:T(2,128)} %param.11) | copy-start | bytes 6148
  10.5 19.9 %collective-permute-start = (f32[512,64]{1,0:T(8,128)}, f32[512,64]{1,0:T(8,128)}, u32[]{:S(2)}, u32[]{:S(2)}) collective-permute-start(f32[512,64]{1,0:T(8,128)} %get-tuple-element.17), channel_id=1, source_target_pairs={{8,0},{12,4},{16,8},{20,12},{24,16},{28,20},{9,1},{13,5},{17,9},{2... | collective-permute-start | bytes 393224 | tf_op jit(solution)/shard_map/ppermute | solution.py:17
  11.7 20.9 %collective-permute-start.1 = (f32[512,64]{1,0:T(8,128)}, f32[512,64]{1,0:T(8,128)}, u32[]{:S(2)}, u32[]{:S(2)}) collective-permute-start(f32[512,64]{1,0:T(8,128)} %get-tuple-element.16), channel_id=1, source_target_pairs={{4,0},{8,4},{12,8},{16,12},{20,16},{24,20},{28,24},{5,1},{9,5},{13... | collective-permute-start | bytes 393224 | tf_op jit(solution)/shard_map/ppermute | solution.py:17
  13.0 20.6 %collective-permute-start.2 = (f32[512,64]{1,0:T(8,128)}, f32[512,64]{1,0:T(8,128)}, u32[]{:S(2)}, u32[]{:S(2)}) collective-permute-start(f32[512,64]{1,0:T(8,128)} %get-tuple-element.15), channel_id=1, source_target_pairs={{0,4},{4,8},{8,12},{12,16},{16,20},{20,24},{24,28},{1,5},{5,9},{9,... | collective-permute-start | bytes 393224 | tf_op jit(solution)/shard_map/ppermute | solution.py:17
  19.2 15.4 %collective-permute-start.3 = (f32[512,64]{1,0:T(8,128)}, f32[512,64]{1,0:T(8,128)S(1)}, u32[]{:S(2)}, u32[]{:S(2)}) collective-permute-start(f32[512,64]{1,0:T(8,128)} %get-tuple-element.14), channel_id=1, source_target_pairs={{0,8},{4,12},{8,16},{12,20},{16,24},{20,28},{1,9},{5,13},{9,17},{1... | collective-permute-start | bytes 393224 | tf_op jit(solution)/shard_map/ppermute | solution.py:17
  23.2 4.0 %copy-start.1 = (s32[27,1024]{1,0:T(8,128)S(1)}, s32[27,1024]{1,0:T(8,128)}, u32[]{:S(2)}) copy-start(s32[27,1024]{1,0:T(8,128)} %param.8) | copy-start | bytes 331780
  24.3 3.6 %copy-start.3 = (s32[1,1,4,512]{3,2,1,0:T(4,128)S(1)}, s32[1,1,4,512]{3,2,1,0:T(4,128)}, u32[]{:S(2)}) copy-start(s32[1,1,4,512]{3,2,1,0:T(4,128)} %param.9) | copy-start | bytes 24580
  25.2 9.5 %collective-permute-start.4 = (f32[1,256,64]{2,1,0:T(8,128)}, f32[1,256,64]{2,1,0:T(8,128)}, u32[]{:S(2)}, u32[]{:S(2)}) collective-permute-start(f32[1,256,64]{2,1,0:T(8,128)} %get-tuple-element.19), channel_id=1, source_target_pairs={{0,1},{1,2},{2,3},{4,5},{5,6},{6,7},{8,9},{9,10},{10,11},{12,13},{... | collective-permute-start | bytes 196616 | tf_op jit(solution)/shard_map/ppermute | solution.py:27
  30.4 5.2 %collective-permute-start.5 = (f32[1,256,64]{2,1,0:T(8,128)}, f32[1,256,64]{2,1,0:T(8,128)S(1)}, u32[]{:S(2)}, u32[]{:S(2)}) collective-permute-start(f32[1,256,64]{2,1,0:T(8,128)} %get-tuple-element.18), channel_id=1, source_target_pairs={{1,0},{2,1},{3,2},{5,4},{6,5},{7,6},{9,8},{10,9},{11,10},{13,12},{... | collective-permute-start | bytes 196616 | tf_op jit(solution)/shard_map/ppermute | solution.py:28
  138.9 8.4 %copy-start.2 = (f32[64,1024]{1,0:T(8,128)S(1)}, f32[64,1024]{1,0:T(8,128)}, u32[]{:S(2)}) copy-start(f32[64,1024]{1,0:T(8,128)} %param.7) | copy-start | bytes 786436
  313.4 11.0 %copy-start = (f32[3585,64]{1,0:T(8,128)}, f32[3585,64]{1,0:T(8,128)S(1)}, u32[]{:S(2)}) copy-start(f32[3585,64]{1,0:T(8,128)S(1)} %scatter_custom_fusion) | copy-start | bytes 2753284
  313.4 16.7 %copy-start.6 = (f32[1,512]{1,0:T(1,128)S(1)}, f32[1,512]{1,0:T(1,128)}, u32[]{:S(2)}) copy-start(f32[1,512]{1,0:T(1,128)} %get-tuple-element.23) | copy-start | bytes 6148
  313.4 16.8 %copy-start.5 = (f32[1,512]{1,0:T(1,128)S(1)}, f32[1,512]{1,0:T(1,128)}, u32[]{:S(2)}) copy-start(f32[1,512]{1,0:T(1,128)} %get-tuple-element.22) | copy-start | bytes 6148
  313.5 15.2 %collective-permute-start.6 = (f32[512,64]{1,0:T(8,128)S(1)}, f32[512,64]{1,0:T(8,128)S(1)}, u32[]{:S(2)}, u32[]{:S(2)}) collective-permute-start(f32[512,64]{1,0:T(8,128)S(1)} %get-tuple-element.13), channel_id=1, source_target_pairs={{0,8},{4,12},{8,16},{12,20},{16,24},{20,28},{1,9},{5,13},{9,17},{1... | collective-permute-start | bytes 393224 | tf_op jit(solution)/shard_map/ppermute | solution.py:17
  317.4 12.8 %collective-permute-start.7 = (f32[512,64]{1,0:T(8,128)S(1)}, f32[512,64]{1,0:T(8,128)S(1)}, u32[]{:S(2)}, u32[]{:S(2)}) collective-permute-start(f32[512,64]{1,0:T(8,128)S(1)} %get-tuple-element.12), channel_id=1, source_target_pairs={{0,4},{4,8},{8,12},{12,16},{16,20},{20,24},{24,28},{1,5},{5,9},{9,... | collective-permute-start | bytes 393224 | tf_op jit(solution)/shard_map/ppermute | solution.py:17
  321.8 9.4 %collective-permute-start.8 = (f32[512,64]{1,0:T(8,128)S(1)}, f32[512,64]{1,0:T(8,128)S(1)}, u32[]{:S(2)}, u32[]{:S(2)}) collective-permute-start(f32[512,64]{1,0:T(8,128)S(1)} %get-tuple-element.11), channel_id=1, source_target_pairs={{4,0},{8,4},{12,8},{16,12},{20,16},{24,20},{28,24},{5,1},{9,5},{13... | collective-permute-start | bytes 393224 | tf_op jit(solution)/shard_map/ppermute | solution.py:17
  323.1 15.5 %collective-permute-start.9 = (f32[512,64]{1,0:T(8,128)S(1)}, f32[512,64]{1,0:T(8,128)S(1)}, u32[]{:S(2)}, u32[]{:S(2)}) collective-permute-start(f32[512,64]{1,0:T(8,128)S(1)} %get-tuple-element.10), channel_id=1, source_target_pairs={{8,0},{12,4},{16,8},{20,12},{24,16},{28,20},{9,1},{13,5},{17,9},{2... | collective-permute-start | bytes 393224 | tf_op jit(solution)/shard_map/ppermute | solution.py:17
  324.4 14.3 %collective-permute-start.10 = (f32[1,256,64]{2,1,0:T(8,128)S(1)}, f32[1,256,64]{2,1,0:T(8,128)S(1)}, u32[]{:S(2)}, u32[]{:S(2)}) collective-permute-start(f32[1,256,64]{2,1,0:T(8,128)S(1)} %get-tuple-element.9), channel_id=1, source_target_pairs={{0,1},{1,2},{2,3},{4,5},{5,6},{6,7},{8,9},{9,10},{10,11},{12,13},{... | collective-permute-start | bytes 196616 | tf_op jit(solution)/shard_map/ppermute | solution.py:27
  328.6 10.1 %slice-start = ((f32[3585,64]{1,0:T(8,128)}), f32[1024,64]{1,0:T(8,128)S(1)}, s32[]{:S(2)}) async-start(f32[3585,64]{1,0:T(8,128)} %copy-done), calls=%async_computation | async-start | bytes 1048576 | tf_op jit(solution)/shard_map/slice | solution.py:83
  328.7 10.1 %collective-permute-start.11 = (f32[1,256,64]{2,1,0:T(8,128)S(1)}, f32[1,256,64]{2,1,0:T(8,128)S(1)}, u32[]{:S(2)}, u32[]{:S(2)}) collective-permute-start(f32[1,256,64]{2,1,0:T(8,128)S(1)} %get-tuple-element.8), channel_id=1, source_target_pairs={{1,0},{2,1},{3,2},{5,4},{6,5},{7,6},{9,8},{10,9},{11,10},{13,12},{... | collective-permute-start | bytes 196616 | tf_op jit(solution)/shard_map/ppermute | solution.py:28
where the time goes:
time: 356 us; the launch traced here: 354 us
  other arithmetic  167 us (47%)
  local copies, waits for them, and re-layouts  129 us (36%)
  starting transfers between devices  32.4 us (9%)
  matrix products  16.4 us (5%)
  waiting for transfers between devices  8.08 us (2%)
    scatter-add x1, other arithmetic, local_rows(): jnp.zeros((width, 64), jnp.float32).at[link_table.reshape(-1)]  148 us
    gather x2, local copies, waits for them, and re-layouts, local_rows(): picked = jnp.take(ext_rows, link_table, axis=0)  103 us
    ppermute x8, starting transfers between devices, passed_along(): return lax.ppermute(shard, axis, pairs)  23.5 us
    scatter-add x1, other arithmetic, on_device(): sens = sens.at[jnp.concatenate(places)].add(jnp.concatenate(values, axis=0))  14.4 us
    reshape x1, local copies, waits for them, and re-layouts, local_rows(): spread.reshape(-1, 64)  10.7 us
    dot_general x1, matrix products, local_rows(): jnp.einsum('kbj,kij->bi', picked, table, precision=lax.Precision.HIGHEST)  8.37 us
    ppermute x8, waiting for transfers between devices, passed_along(): return lax.ppermute(shard, axis, pairs)  8.06 us
    dot_general x1, matrix products, local_rows(): jnp.einsum('bi,kij->kbj', scaled, table, precision=lax.Precision.HIGHEST)  7.75 us
  transfers between devices with their start and end apart: 12, of which 2 were waited for; matrix products, arithmetic and copies ran while one was open for 3% of the time, Pallas kernels for 0%

commit v1 on v0

v1 whole, which is shorter than its diff:
```python
import functools

import jax
import jax.numpy as jnp
import numpy as np
from jax import lax
from jax.experimental import pallas as pl
from jax.experimental.pallas import tpu as pltpu
from jax.sharding import PartitionSpec as P

REACH = 2
OFFSETS = [o for o in range(-REACH, REACH + 1) if o != 0]
RADIUS = 3.0
FLOOR = 0.001
PENALTY = 3.0
LO = 256
BF = jnp.bfloat16
F32 = jnp.float32


def cone_table():
    v = np.arange(64)
    place = np.stack([v // 16, v // 4 % 4, v % 4], -1).astype(np.float32)
    k = np.arange(27)
    moved = np.stack([k // 9 - 1, k // 3 % 3 - 1, k % 3 - 1], -1).astype(np.float32) * 4
    apart = place[None, :, None] - place[None, None] - moved[:, None, None]
    return np.maximum(
        np.float32(0), np.float32(RADIUS) - np.sqrt(np.sum(apart * apart, -1, dtype=np.float32))
    ).astype(np.float32)


def split_np(a, terms):
    out = []
    for _ in range(terms):
        part = a.astype(jnp.bfloat16)
        out.append(part)
        a = (a - part.astype(np.float32)).astype(np.float32)
    return out


W = cone_table()
USED = [np.nonzero(W[k].any(0))[0] for k in range(27)]
CORNERS = [k for k in range(27) if len(USED[k]) == 4]
EDGES = [k for k in range(27) if len(USED[k]) == 16]
FACES = [k for k in range(27) if len(USED[k]) == 32]
ORDER = CORNERS + EDGES + FACES
NC, NE, NF = len(CORNERS), len(EDGES), len(FACES)
C_ROWS, E_ROWS, F_ROWS = 8 * NC, 16 * NE, 32 * NF
E_AT, F_AT = C_ROWS, C_ROWS + E_ROWS
M_AT = F_AT + F_ROWS
ALL_ROWS = M_AT + 64


def constants():
    pick = np.zeros((C_ROWS + 2 * E_ROWS + 2 * F_ROWS, 128), np.float32)
    conv = np.zeros((64, ALL_ROWS), np.float32)
    back = np.zeros((ALL_ROWS, 64), np.float32)
    put = np.zeros((64, M_AT), np.float32)
    for i, k in enumerate(CORNERS):
        for r, j in enumerate(USED[k]):
            pick[8 * i + r, j] = 1
            pick[8 * i + 4 + r, 64 + j] = 1
            for row in (8 * i + r, 8 * i + 4 + r):
                conv[:, row] = W[k][:, j]
                back[row] = W[k][:, j]
                put[j, row] = 1
    for kinds, size, at, src in (
        (EDGES, 16, E_AT, C_ROWS),
        (FACES, 32, F_AT, C_ROWS + 2 * E_ROWS),
    ):
        for i, k in enumerate(kinds):
            for r, j in enumerate(USED[k]):
                pick[src + size * i + r, j] = 1
                pick[src + size * len(kinds) + size * i + r, 64 + j] = 1
                row = at + size * i + r
                conv[:, row] = W[k][:, j]
                back[row] = W[k][:, j]
                put[j, row] = 1
    conv[:, M_AT:] = W[13]
    back[M_AT:] = W[13].T
    sums = np.zeros((64, 32), np.float32)
    for i, k in enumerate(ORDER + [13]):
        sums[:, i] = W[k].sum(1, dtype=np.float32)
    conv_hi, conv_lo = split_np(conv, 2)
    back_hi, back_lo = split_np(back, 2)
    return (
        pick.astype(jnp.bfloat16),
        np.concatenate([conv_hi, conv_lo], 0),
        np.concatenate([back_hi, back_hi, back_lo], 1),
        put.astype(jnp.bfloat16),
        np.concatenate(split_np(sums, 3), 0),
    )


def dot(a, b):
    return jnp.dot(a, b, preferred_element_type=F32)


def dot_t(a, b):
    return lax.dot_general(a, b, (((1,), (1,)), ((), ())), preferred_element_type=F32)


def halves(x):
    hi = x.astype(BF)
    return hi, (x - hi.astype(F32)).astype(BF)


def one_hot(rows, index):
    at = lax.broadcasted_iota(jnp.int32, (rows, index.shape[1]), 0)
    return jnp.where(at == index, 1.0, 0.0).astype(BF)


def listed(index_ref, live_ref, face_ref, chunk):
    if chunk < 8:
        group, half = chunk // 2, chunk % 2
        index = index_ref[0, 0, group : group + 1, half * LO : (half + 1) * LO]
        slot = lax.broadcasted_iota(jnp.int32, (1, LO), 1) + half * LO
        return jnp.where(slot < live_ref[0, 0, group], index, -1)
    return face_ref[0, 0, chunk - 8 : chunk - 7, :]


def pack_stage(x_ref, index_ref, live_ref, face_ref, pay_ref):
    rows = jnp.concatenate(halves(x_ref[...]), 0)
    for chunk in range(10):
        spot = one_hot(x_ref.shape[1], listed(index_ref, live_ref, face_ref, chunk))
        both = dot(rows, spot)
        pay_ref[chunk] = both[:64] + both[64:]


def links_stage(links_ref, lo_ref, hi_ref, valid_ref):
    columns = links_ref.shape[1]
    for i, k in enumerate(ORDER):
        row = links_ref[k : k + 1, :]
        lo_ref[i] = row & (LO - 1)
        hi_ref[i] = row >> 8
        valid_ref[i : i + 1, :] = jnp.where(row != 14 * LO, 1.0, 0.0)
    valid_ref[26:27, :] = jnp.ones((1, columns), F32)
    valid_ref[27:32, :] = jnp.zeros((5, columns), F32)


def pick_stage(chunk, h, pick_ref, lc, le, lf):
    out = dot(pick_ref[...], jnp.concatenate(halves(chunk), 0))
    for i in range(NC):
        lc[i, pl.ds(pl.multiple_of(h * 8, 8), 8), :] = out[8 * i : 8 * i + 8]
    for src, size, count, ref in ((C_ROWS, 16, NE, le), (C_ROWS + 2 * E_ROWS, 32, NF, lf)):
        to = pl.ds(pl.multiple_of(h * size, size), size)
        for i in range(count):
            at = src + size * i
            ref[i, to, 0:LO] = out[at : at + size].astype(BF)
            at = at + size * count
            ref[i, to, LO : 2 * LO] = out[at : at + size].astype(BF)


def gather_stage(first, count, size, at, src_ref, lo_ref, hi_ref, hot_ref, g_ref):
    def body(i, carry):
        spot = one_hot(LO, lo_ref[first + i])
        hot_ref[first + i] = spot
        columns = spot.shape[1]
        if size == 8:
            out = dot(src_ref[i].astype(BF), spot)
        else:
            out = dot(src_ref[i], jnp.concatenate([spot, spot], 0))
        hi = jnp.broadcast_to(hi_ref[first + i], (8, columns))
        acc = [jnp.zeros((8, columns), F32) for _ in range(size // 8)]
        for h in range(14):
            here = hi == h
            for r in range(size // 8):
                row = h * size + r * 8
                acc[r] = jnp.where(here, out[row : row + 8], acc[r])
        for r in range(size // 8):
            g_ref[pl.ds(pl.multiple_of(at + size * i + 8 * r, 8), 8), :] = acc[r]
        return carry

    lax.fori_loop(0, count, body, 0)


def filter_stage(energy_ref, conv_ref, back_ref, sums_ref, valid_ref, g_ref, cond_ref, sc, se, sf, mid_ref):
    g_hi, g_lo = halves(g_ref[...])
    conv = conv_ref[...]
    main = dot(conv, g_hi)
    total = main[:64] + main[64:] + dot(conv[:64], g_lo)
    hs = dot(sums_ref[...], valid_ref[...].astype(BF))
    hs = hs[:64] + hs[64:128] + hs[128:]
    filtered = total / hs
    square = filtered * filtered
    cond_ref[...] = FLOOR + square * filtered * (1.0 - FLOOR)
    scaled = -PENALTY * (1.0 - FLOOR) * square * energy_ref[...] / hs
    s_hi, s_lo = halves(scaled)
    spread = dot(back_ref[...], jnp.concatenate([s_hi, s_lo, s_hi], 0))
    low_half = lax.broadcasted_iota(jnp.int32, (8, spread.shape[1]), 0) < 4
    for i in range(NC):
        part = spread[8 * i : 8 * i + 8]
        rounded = part.astype(BF).astype(F32)
        sc[i] = jnp.where(low_half, rounded, part - rounded)
    for at, size, count, ref in ((E_AT, 16, NE, se), (F_AT, 32, NF, sf)):
        for i in range(count):
            hi, lo = halves(spread[at + size * i : at + size * (i + 1)])
            ref[i, 0:size, :] = hi
            ref[i, size : 2 * size, :] = lo
    mid_ref[...] = spread[M_AT:]


def scatter_stage(first, count, size, at, src_ref, hi_ref, hot_ref, d_ref, chunks):
    def body(i, carry):
        spot = hot_ref[first + i]
        columns = spot.shape[1]
        rows = src_ref[i]
        pieces = []
        if size == 8:
            hi = jnp.broadcast_to(hi_ref[first + i], (8, columns))
            for h in chunks:
                pieces.append(jnp.where(hi == h, rows, 0.0))
            left = jnp.concatenate(pieces, 0).astype(BF)
        else:
            hi = jnp.broadcast_to(hi_ref[first + i], (16, columns))
            for h in chunks:
                here = jnp.where(hi == h, 1.0, 0.0).astype(BF)
                for r in range(size // 8):
                    pieces.append(rows[16 * r : 16 * r + 16] * here)
            left = jnp.concatenate(pieces, 0)
        out = dot_t(left, spot)
        to = pl.ds(pl.multiple_of(at + size * i, 8), size)
        for n, h in enumerate(chunks):
            if size == 8:
                d_ref[h, to, :] = out[8 * n : 8 * n + 8]
            else:
                row = 2 * size * n
                d_ref[h, to, :] = out[row : row + size] + out[row + size : row + 2 * size]
        return carry

    lax.fori_loop(0, count, body, 0)


def put_stage(h, put_ref, d_ref):
    hi, lo = halves(d_ref[h])
    return dot(put_ref[...], hi) + dot(put_ref[...], lo)


def finish_stage(index_ref, live_ref, face_ref, sens, back_chunk):
    total = jnp.zeros((128, sens.shape[1]), F32)
    for chunk in range(10):
        spot = one_hot(sens.shape[1], listed(index_ref, live_ref, face_ref, chunk))
        total = total + dot_t(jnp.concatenate(halves(back_chunk(chunk)), 0), spot)
    return sens + total[:64] + total[64:]


def main_kernel(
    x_ref, energy_ref, links_ref, r0, r1, r2, r3, low_ref, up_ref,
    pick_ref, conv_ref, back_ref, put_ref, sums_ref,
    cond_ref, sens_ref, b0, b1, b2, b3, blow_ref, bup_ref,
    lo_ref, hi_ref, valid_ref, lc, le, lf, hot_ref, g_ref, sc, se, sf, mid_ref, d_ref,
):
    links_stage(links_ref, lo_ref, hi_ref, valid_ref)
    got = (r0, r1, r2, r3)
    sent = (b0, b1, b2, b3)
    for h in range(14):
        if h < 4:
            chunk = x_ref[:, h * LO : (h + 1) * LO]
        elif h < 12:
            chunk = got[(h - 4) // 2][h % 2]
        else:
            chunk = (low_ref if h == 12 else up_ref)[...]
        pick_stage(chunk, h, pick_ref, lc, le, lf)
    gather_stage(0, NC, 8, 0, lc, lo_ref, hi_ref, hot_ref, g_ref)
    gather_stage(NC, NE, 16, E_AT, le, lo_ref, hi_ref, hot_ref, g_ref)
    gather_stage(NC + NE, NF, 32, F_AT, lf, lo_ref, hi_ref, hot_ref, g_ref)
    g_ref[M_AT:, :] = x_ref[...]
    filter_stage(energy_ref, conv_ref, back_ref, sums_ref, valid_ref, g_ref, cond_ref, sc, se, sf, mid_ref)
    chunks = list(range(14))
    scatter_stage(0, NC, 8, 0, sc, hi_ref, hot_ref, d_ref, chunks)
    scatter_stage(NC, NE, 16, E_AT, se, hi_ref, hot_ref, d_ref, chunks)
    scatter_stage(NC + NE, NF, 32, F_AT, sf, hi_ref, hot_ref, d_ref, chunks)
    for h in range(14):
        part = put_stage(h, put_ref, d_ref)
        if h < 4:
            columns = slice(h * LO, (h + 1) * LO)
            sens_ref[:, columns] = part + mid_ref[:, columns]
        elif h < 12:
            sent[(h - 4) // 2][h % 2] = part
        else:
            (blow_ref if h == 12 else bup_ref)[...] = part


def final_kernel(sens_ref, r0, r1, r2, r3, f0, f1, index_ref, live_ref, face_ref, out_ref):
    got = (r0, r1, r2, r3)

    def back_chunk(chunk):
        if chunk < 8:
            return got[chunk // 2][chunk % 2]
        return (f0 if chunk == 8 else f1)[...]

    out_ref[...] = finish_stage(index_ref, live_ref, face_ref, sens_ref[...], back_chunk)


def moved(shard, axis, by):
    count = lax.axis_size(axis)
    return lax.ppermute(shard, axis, [(i, i + by) for i in range(count) if 0 <= i + by < count])


VM = pl.BlockSpec(memory_space=pltpu.VMEM)
SM = pl.BlockSpec(memory_space=pltpu.SMEM)
PARAMS = pltpu.CompilerParams(vmem_limit_bytes=56 * 1024 * 1024)


def shape(*dims):
    return jax.ShapeDtypeStruct(dims, F32)


def on_device(density, energy, links, send_index, send_live, face_index):
    blocks = density.shape[1]
    consts = [jnp.asarray(c) for c in constants()]
    pay = pl.pallas_call(
        pack_stage,
        out_shape=shape(10, 64, LO),
        in_specs=[VM, VM, SM, VM],
        out_specs=VM,
        compiler_params=PARAMS,
    )(density, send_index, send_live, face_index)
    got = [moved(pay[2 * g : 2 * g + 2], "plane", o) for g, o in enumerate(OFFSETS)]
    up = moved(pay[8], "depth", -1)
    low = moved(pay[9], "depth", 1)
    outs = pl.pallas_call(
        main_kernel,
        out_shape=[shape(64, blocks)] * 2 + [shape(2, 64, LO)] * 4 + [shape(64, LO)] * 2,
        in_specs=[VM] * 14,
        out_specs=[VM] * 8,
        scratch_shapes=[
            pltpu.VMEM((26, 1, blocks), jnp.int32),
            pltpu.VMEM((26, 1, blocks), jnp.int32),
            pltpu.VMEM((32, blocks), F32),
            pltpu.VMEM((NC, 14 * 8, LO), F32),
            pltpu.VMEM((NE, 14 * 16, 2 * LO), BF),
            pltpu.VMEM((NF, 14 * 32, 2 * LO), BF),
            pltpu.VMEM((26, LO, blocks), BF),
            pltpu.VMEM((ALL_ROWS, blocks), F32),
            pltpu.VMEM((NC, 8, blocks), F32),
            pltpu.VMEM((NE, 32, blocks), BF),
            pltpu.VMEM((NF, 64, blocks), BF),
            pltpu.VMEM((64, blocks), F32),
            pltpu.VMEM((14, M_AT, LO), F32),
        ],
        compiler_params=PARAMS,
    )(density, energy, links, *got, low, up, *consts)
    cond, sens = outs[:2]
    returned = [moved(outs[2 + g], "plane", -o) for g, o in enumerate(OFFSETS)]
    face_1 = moved(outs[6], "depth", -1)
    face_0 = moved(outs[7], "depth", 1)
    sens = pl.pallas_call(
        final_kernel,
        out_shape=shape(64, blocks),
        in_specs=[VM] * 8 + [SM, VM],
        out_specs=VM,
        compiler_params=PARAMS,
    )(sens, *returned, face_0, face_1, send_index, send_live, face_index)
    return cond, sens


def solution(mesh):
    in_specs = (
        P(None, ("plane", "depth")),
        P(None, ("plane", "depth")),
        P(None, ("plane", "depth")),
        P("plane", "depth", None, None),
        P("plane", "depth", None),
        P("plane", "depth", None, None),
    )
    out_specs = (P(None, ("plane", "depth")), P(None, ("plane", "depth")))
    return jax.shard_map(
        on_device, mesh=mesh, in_specs=in_specs, out_specs=out_specs, check_vma=False
    )
```

time: 356 us -> 84.8 us (0.24)
  other arithmetic: 167 us -> 0 us
  local copies, waits for them, and re-layouts: 129 us -> 3.31 us
  Pallas kernels: 0 us -> 38.2 us
  matrix products: 16.4 us -> 0 us
  waiting for transfers between devices: 8.08 us -> 14.9 us
  starting transfers between devices: 32.4 us -> 26.8 us
    scatter-add x2 -> x0, other arithmetic: 162 us -> none  [the longest x1 148 us: local_rows(): jnp.zeros((width, 64), jnp.float32).at[link_table.reshape(-1)]]
    gather x4 -> x0, local copies, waits for them, and re-layouts: 110 us -> none  [the longest x2 103 us: local_rows(): picked = jnp.take(ext_rows, link_table, axis=0)]
    pallas_call x0 -> x3, Pallas kernels: none -> 38.2 us  [the longest x1 31.7 us: on_device(): pl.pallas_call(main_kernel, out_shape=[shape(64, blocks)] * 2 + [shape(2,...]
    dot_general x3 -> x0, matrix products: 16.4 us -> none  [the longest x1 8.37 us: local_rows(): jnp.einsum('kbj,kij->bi', picked, table, precision=lax.Precision.HIGHEST)]
    reshape x1 -> x0, local copies, waits for them, and re-layouts: 10.7 us -> none  [local_rows(): spread.reshape(-1, 64)]
    ppermute x12, waiting for transfers between devices: 8.08 us -> 14.9 us  [moved(): lax.ppermute(shard, axis, [(i, i + by) for i in range(count) if 0 <= i +...]
    ppermute x12, starting transfers between devices: 32.4 us -> 26.8 us  [moved(): lax.ppermute(shard, axis, [(i, i + by) for i in range(count) if 0 <= i +...]
    unnamed x32 -> x24, local copies, waits for them, and re-layouts: 6.13 us -> 1.3 us
  transfers between devices with their start and end apart: 12 -> 12, of which waited for: 2 -> 6; matrix products, arithmetic and copies ran while one was open for 3% -> 1% of each run, Pallas kernels for 0% -> 0%
where the time goes in v1:
time: 84.8 us; the launch traced here: 84.1 us
  Pallas kernels  38.2 us (45%)
  starting transfers between devices  26.8 us (32%)
  waiting for transfers between devices  14.9 us (18%)
  local copies, waits for them, and re-layouts  3.31 us (4%)
    pallas_call x1, Pallas kernels, on_device(): pl.pallas_call(main_kernel, out_shape=[shape(64, blocks)] * 2 + [shape(2,...  31.7 us
    ppermute x12, starting transfers between devices, moved(): lax.ppermute(shard, axis, [(i, i + by) for i in range(count) if 0 <= i +...  26.8 us
    ppermute x12, waiting for transfers between devices, moved(): lax.ppermute(shard, axis, [(i, i + by) for i in range(count) if 0 <= i +...  14.9 us
    pallas_call x1, Pallas kernels, on_device(): pl.pallas_call(final_kernel, out_shape=shape(64, blocks), in_specs=[VM] *...  3.79 us
    pallas_call x1, Pallas kernels, on_device(): pl.pallas_call(pack_stage, out_shape=shape(10, 64, LO), in_specs=[VM, VM,...  2.71 us
  transfers between devices with their start and end apart: 12, of which 6 were waited for; matrix products, arithmetic and copies ran while one was open for 1% of the time, Pallas kernels for 0%

profile of v1, /device:TPU:0, one launch (start us, length us, event | category | flops | bytes accessed | tf_op | source)
XLA Modules:
  0.0 84.1 jit_solution(5105545360773133360)
XLA Ops:
  0.6 2.7 %shard_map.122 = f32[10,64,256]{2,1,0:T(8,128)} custom-call(f32[64,1024]{1,0:T(8,128)} %x_ref.3, s32[1,1,4,512]{3,2,1,0:T(4,128)} %index_ref.3, s32[1,1,4]{2,1,0:T(1,128)} %live_ref.3, s32[1,1,2,256]{3,2,1,0:T(2,128)} %face_ref.3), custom_call_target="tpu_custom_call" | custom-call | tf_op jit(solution)/shard_map/pallas_call | solution.py:312
  3.3 0.9 %slice_bitcast_fusion = (f32[64,256]{1,0:T(8,128)S(1)}, f32[64,256]{1,0:T(8,128)S(1)}) fusion(f32[10,64,256]{2,1,0:T(8,128)} %shard_map.122), kind=kLoop, calls=%fused_computation | loop fusion | bytes 262144 | tf_op jit(solution)/shard_map/squeeze | solution.py:320
  4.2 1.3 %collective-permute-start.5 = (f32[64,256]{1,0:T(8,128)S(1)}, f32[64,256]{1,0:T(8,128)S(1)}, u32[]{:S(2)}, u32[]{:S(2)}) collective-permute-start(f32[64,256]{1,0:T(8,128)S(1)} %get-tuple-element.18), channel_id=1, source_target_pairs={{1,0},{2,1},{3,2},{5,4},{6,5},{7,6},{9,8},{10,9},{11,10},{13,12},{... | collective-permute-start | bytes 196616 | tf_op jit(solution)/shard_map/ppermute | solution.py:297
  5.5 1.1 %fusion = (f32[2,64,256]{2,1,0:T(8,128)S(1)}, f32[2,64,256]{2,1,0:T(8,128)S(1)}, f32[2,64,256]{2,1,0:T(8,128)S(1)}, f32[2,64,256]{2,1,0:T(8,128)S(1)}) fusion(f32[10,64,256]{2,1,0:T(8,128)} %shard_map.122), kind=kLoop, calls=%fused_computation.2 | loop fusion | bytes 1048576 | tf_op jit(solution)/shard_map/slice | solution.py:319
  6.7 4.9 %collective-permute-start.3 = (f32[2,64,256]{2,1,0:T(8,128)S(1)}, f32[2,64,256]{2,1,0:T(8,128)S(1)}, u32[]{:S(2)}, u32[]{:S(2)}) collective-permute-start(f32[2,64,256]{2,1,0:T(8,128)S(1)} %get-tuple-element.20), channel_id=1, source_target_pairs={{0,8},{4,12},{8,16},{12,20},{16,24},{20,28},{1,9},{5,13},{9,17},{1... | collective-permute-start | bytes 393224 | tf_op jit(solution)/shard_map/ppermute | solution.py:297
  11.6 3.4 %collective-permute-start.2 = (f32[2,64,256]{2,1,0:T(8,128)S(1)}, f32[2,64,256]{2,1,0:T(8,128)S(1)}, u32[]{:S(2)}, u32[]{:S(2)}) collective-permute-start(f32[2,64,256]{2,1,0:T(8,128)S(1)} %get-tuple-element.21), channel_id=1, source_target_pairs={{0,4},{4,8},{8,12},{12,16},{16,20},{20,24},{24,28},{1,5},{5,9},{9,... | collective-permute-start | bytes 393224 | tf_op jit(solution)/shard_map/ppermute | solution.py:297
  15.0 1.3 %collective-permute-start.1 = (f32[2,64,256]{2,1,0:T(8,128)S(1)}, f32[2,64,256]{2,1,0:T(8,128)S(1)}, u32[]{:S(2)}, u32[]{:S(2)}) collective-permute-start(f32[2,64,256]{2,1,0:T(8,128)S(1)} %get-tuple-element.22), channel_id=1, source_target_pairs={{4,0},{8,4},{12,8},{16,12},{20,16},{24,20},{28,24},{5,1},{9,5},{13... | collective-permute-start | bytes 393224 | tf_op jit(solution)/shard_map/ppermute | solution.py:297
  16.3 1.3 %collective-permute-start = (f32[2,64,256]{2,1,0:T(8,128)S(1)}, f32[2,64,256]{2,1,0:T(8,128)S(1)}, u32[]{:S(2)}, u32[]{:S(2)}) collective-permute-start(f32[2,64,256]{2,1,0:T(8,128)S(1)} %get-tuple-element.23), channel_id=1, source_target_pairs={{8,0},{12,4},{16,8},{20,12},{24,16},{28,20},{9,1},{13,5},{17,9},{2... | collective-permute-start | bytes 393224 | tf_op jit(solution)/shard_map/ppermute | solution.py:297
  17.6 0.0 collective-permute-done.5.up_ref
  17.6 0.0 copy-start.8
  17.6 2.5 %collective-permute-start.4 = (f32[64,256]{1,0:T(8,128)S(1)}, f32[64,256]{1,0:T(8,128)S(1)}, u32[]{:S(2)}, u32[]{:S(2)}) collective-permute-start(f32[64,256]{1,0:T(8,128)S(1)} %get-tuple-element.19), channel_id=1, source_target_pairs={{0,1},{1,2},{2,3},{4,5},{5,6},{6,7},{8,9},{9,10},{10,11},{12,13},{... | collective-permute-start | bytes 196616 | tf_op jit(solution)/shard_map/ppermute | solution.py:297
  20.1 0.9 %collective-permute-done.4.low_ref = f32[64,256]{1,0:T(8,128)S(1)} collective-permute-done((f32[64,256]{1,0:T(8,128)S(1)}, f32[64,256]{1,0:T(8,128)S(1)}, u32[]{:S(2)}, u32[]{:S(2)}) %collective-permute-start.4) | collective-permute-done | bytes 65568 | tf_op jit(solution)/shard_map/ppermute | solution.py:297
  21.0 0.0 copy-start.10
  21.0 0.0 collective-permute-done.3.r3
  21.0 0.0 copy-start
  21.0 0.0 collective-permute-done.2.r2
  21.0 0.0 copy-start.1
  21.0 1.9 %collective-permute-done.1.r1 = f32[2,64,256]{2,1,0:T(8,128)S(1)} collective-permute-done((f32[2,64,256]{2,1,0:T(8,128)S(1)}, f32[2,64,256]{2,1,0:T(8,128)S(1)}, u32[]{:S(2)}, u32[]{:S(2)}) %collective-permute-start.1) | collective-permute-done | bytes 131104 | tf_op jit(solution)/shard_map/ppermute | solution.py:297
  22.9 3.8 %collective-permute-done.r0 = f32[2,64,256]{2,1,0:T(8,128)S(1)} collective-permute-done((f32[2,64,256]{2,1,0:T(8,128)S(1)}, f32[2,64,256]{2,1,0:T(8,128)S(1)}, u32[]{:S(2)}, u32[]{:S(2)}) %collective-permute-start) | collective-permute-done | bytes 131104 | tf_op jit(solution)/shard_map/ppermute | solution.py:297
  26.7 0.0 copy-done.8
  26.7 0.0 copy-done.10
  26.7 0.0 copy-done
  26.7 0.0 copy-done.1
  26.7 0.0 copy-done.2
  26.7 0.0 copy-start.3
  26.7 0.6 copy-done.3
  27.3 31.7 %shard_map.123 = (f32[64,1024]{1,0:T(8,128)}, f32[64,1024]{1,0:T(8,128)}, f32[2,64,256]{2,1,0:T(8,128)}, f32[2,64,256]{2,1,0:T(8,128)}, f32[2,64,256]{2,1,0:T(8,...) custom-call(f32[64,1024]{1,0:T(8,128)} %x_ref.3, f32[64,1024]{1,0:T(8,128)} %energy_ref.1, ...), custom_call_target="tpu_custom_call" | custom-call | tf_op jit(solution)/shard_map/pallas_call | solution.py:322
  59.0 1.7 %collective-permute-start.10 = (f32[64,256]{1,0:T(8,128)}, f32[64,256]{1,0:T(8,128)S(1)}, u32[]{:S(2)}, u32[]{:S(2)}) collective-permute-start(f32[64,256]{1,0:T(8,128)} %get-tuple-element.16), channel_id=1, source_target_pairs={{0,1},{1,2},{2,3},{4,5},{5,6},{6,7},{8,9},{9,10},{10,11},{12,13},{... | collective-permute-start | bytes 196616 | tf_op jit(solution)/shard_map/ppermute | solution.py:297
  60.7 3.6 %collective-permute-start.6 = (f32[2,64,256]{2,1,0:T(8,128)}, f32[2,64,256]{2,1,0:T(8,128)S(1)}, u32[]{:S(2)}, u32[]{:S(2)}) collective-permute-start(f32[2,64,256]{2,1,0:T(8,128)} %get-tuple-element.12), channel_id=1, source_target_pairs={{0,8},{4,12},{8,16},{12,20},{16,24},{20,28},{1,9},{5,13},{9,17},{1... | collective-permute-start | bytes 393224 | tf_op jit(solution)/shard_map/ppermute | solution.py:297
  64.3 3.0 %collective-permute-start.7 = (f32[2,64,256]{2,1,0:T(8,128)}, f32[2,64,256]{2,1,0:T(8,128)S(1)}, u32[]{:S(2)}, u32[]{:S(2)}) collective-permute-start(f32[2,64,256]{2,1,0:T(8,128)} %get-tuple-element.13), channel_id=1, source_target_pairs={{0,4},{4,8},{8,12},{12,16},{16,20},{20,24},{24,28},{1,5},{5,9},{9,... | collective-permute-start | bytes 393224 | tf_op jit(solution)/shard_map/ppermute | solution.py:297
  67.3 1.3 %collective-permute-start.8 = (f32[2,64,256]{2,1,0:T(8,128)}, f32[2,64,256]{2,1,0:T(8,128)S(1)}, u32[]{:S(2)}, u32[]{:S(2)}) collective-permute-start(f32[2,64,256]{2,1,0:T(8,128)} %get-tuple-element.14), channel_id=1, source_target_pairs={{4,0},{8,4},{12,8},{16,12},{20,16},{24,20},{28,24},{5,1},{9,5},{13... | collective-permute-start | bytes 393224 | tf_op jit(solution)/shard_map/ppermute | solution.py:297
  68.6 1.3 %collective-permute-start.9 = (f32[2,64,256]{2,1,0:T(8,128)}, f32[2,64,256]{2,1,0:T(8,128)S(1)}, u32[]{:S(2)}, u32[]{:S(2)}) collective-permute-start(f32[2,64,256]{2,1,0:T(8,128)} %get-tuple-element.15), channel_id=1, source_target_pairs={{8,0},{12,4},{16,8},{20,12},{24,16},{28,20},{9,1},{13,5},{17,9},{2... | collective-permute-start | bytes 393224 | tf_op jit(solution)/shard_map/ppermute | solution.py:297
  69.9 0.0 collective-permute-done.10.f0
  69.9 0.0 copy-start.9
  69.9 1.3 %collective-permute-start.11 = (f32[64,256]{1,0:T(8,128)}, f32[64,256]{1,0:T(8,128)S(1)}, u32[]{:S(2)}, u32[]{:S(2)}) collective-permute-start(f32[64,256]{1,0:T(8,128)} %get-tuple-element.17), channel_id=1, source_target_pairs={{1,0},{2,1},{3,2},{5,4},{6,5},{7,6},{9,8},{10,9},{11,10},{13,12},{... | collective-permute-start | bytes 196616 | tf_op jit(solution)/shard_map/ppermute | solution.py:297
  71.2 3.4 %collective-permute-done.11.f1 = f32[64,256]{1,0:T(8,128)S(1)} collective-permute-done((f32[64,256]{1,0:T(8,128)}, f32[64,256]{1,0:T(8,128)S(1)}, u32[]{:S(2)}, u32[]{:S(2)}) %collective-permute-start.11) | collective-permute-done | bytes 65568 | tf_op jit(solution)/shard_map/ppermute | solution.py:297
  74.6 0.0 collective-permute-done.6.r0
  74.6 0.0 collective-permute-done.7.r1
  74.6 0.0 copy-start.5
  74.6 0.5 collective-permute-done.8.r2
  75.1 4.6 %collective-permute-done.9.r3 = f32[2,64,256]{2,1,0:T(8,128)S(1)} collective-permute-done((f32[2,64,256]{2,1,0:T(8,128)}, f32[2,64,256]{2,1,0:T(8,128)S(1)}, u32[]{:S(2)}, u32[]{:S(2)}) %collective-permute-start.9) | collective-permute-done | bytes 131104 | tf_op jit(solution)/shard_map/ppermute | solution.py:297
  79.6 0.0 copy-done.9
  79.6 0.0 copy-done.11
  79.6 0.0 copy-done.4
  79.6 0.0 copy-done.5
  79.7 0.0 copy-done.6
  79.7 0.6 copy-done.7
  80.3 3.8 %shard_map.124 = f32[64,1024]{1,0:T(8,128)} custom-call(f32[64,1024]{1,0:T(8,128)} %get-tuple-element.11.sens_ref, f32[2,64,256]{2,1,0:T(8,128)} %copy-done.4, f32[2,64,256]{2,1,0:T(8,128)} %copy-done.5, f32[2,64,256]{2,1,0:T(8,128)} %copy-done.6, f32[2,64,256]{2,1,0:T(8,128)} %copy-done.7, f32[64,256]{1,0:T(8,128)} %copy-done.9, f32[64,256]{1,0:T(8,128)} %copy-done.11, ...), custom_call_target="tpu_custom_call" | custom-call | tf_op jit(solution)/shard_map/pallas_call | solution.py:348
  (5 shorter events, 0.0 us)
Async XLA Ops:
  4.2 13.4 %collective-permute-start.5 = (f32[64,256]{1,0:T(8,128)S(1)}, f32[64,256]{1,0:T(8,128)S(1)}, u32[]{:S(2)}, u32[]{:S(2)}) collective-permute-start(f32[64,256]{1,0:T(8,128)S(1)} %get-tuple-element.18), channel_id=1, source_target_pairs={{1,0},{2,1},{3,2},{5,4},{6,5},{7,6},{9,8},{10,9},{11,10},{13,12},{... | collective-permute-start | bytes 196616 | tf_op jit(solution)/shard_map/ppermute | solution.py:297
  6.7 14.3 %collective-permute-start.3 = (f32[2,64,256]{2,1,0:T(8,128)S(1)}, f32[2,64,256]{2,1,0:T(8,128)S(1)}, u32[]{:S(2)}, u32[]{:S(2)}) collective-permute-start(f32[2,64,256]{2,1,0:T(8,128)S(1)} %get-tuple-element.20), channel_id=1, source_target_pairs={{0,8},{4,12},{8,16},{12,20},{16,24},{20,28},{1,9},{5,13},{9,17},{1... | collective-permute-start | bytes 393224 | tf_op jit(solution)/shard_map/ppermute | solution.py:297
  11.6 9.4 %collective-permute-start.2 = (f32[2,64,256]{2,1,0:T(8,128)S(1)}, f32[2,64,256]{2,1,0:T(8,128)S(1)}, u32[]{:S(2)}, u32[]{:S(2)}) collective-permute-start(f32[2,64,256]{2,1,0:T(8,128)S(1)} %get-tuple-element.21), channel_id=1, source_target_pairs={{0,4},{4,8},{8,12},{12,16},{16,20},{20,24},{24,28},{1,5},{5,9},{9,... | collective-permute-start | bytes 393224 | tf_op jit(solution)/shard_map/ppermute | solution.py:297
  15.0 7.9 %collective-permute-start.1 = (f32[2,64,256]{2,1,0:T(8,128)S(1)}, f32[2,64,256]{2,1,0:T(8,128)S(1)}, u32[]{:S(2)}, u32[]{:S(2)}) collective-permute-start(f32[2,64,256]{2,1,0:T(8,128)S(1)} %get-tuple-element.22), channel_id=1, source_target_pairs={{4,0},{8,4},{12,8},{16,12},{20,16},{24,20},{28,24},{5,1},{9,5},{13... | collective-permute-start | bytes 393224 | tf_op jit(solution)/shard_map/ppermute | solution.py:297
  16.3 10.3 %collective-permute-start = (f32[2,64,256]{2,1,0:T(8,128)S(1)}, f32[2,64,256]{2,1,0:T(8,128)S(1)}, u32[]{:S(2)}, u32[]{:S(2)}) collective-permute-start(f32[2,64,256]{2,1,0:T(8,128)S(1)} %get-tuple-element.23), channel_id=1, source_target_pairs={{8,0},{12,4},{16,8},{20,12},{24,16},{28,20},{9,1},{13,5},{17,9},{2... | collective-permute-start | bytes 393224 | tf_op jit(solution)/shard_map/ppermute | solution.py:297
  17.6 9.0 %copy-start.8 = (f32[64,256]{1,0:T(8,128)}, f32[64,256]{1,0:T(8,128)S(1)}, u32[]{:S(2)}) copy-start(f32[64,256]{1,0:T(8,128)S(1)} %collective-permute-done.5.up_ref) | copy-start | bytes 196612
  17.6 3.4 %collective-permute-start.4 = (f32[64,256]{1,0:T(8,128)S(1)}, f32[64,256]{1,0:T(8,128)S(1)}, u32[]{:S(2)}, u32[]{:S(2)}) collective-permute-start(f32[64,256]{1,0:T(8,128)S(1)} %get-tuple-element.19), channel_id=1, source_target_pairs={{0,1},{1,2},{2,3},{4,5},{5,6},{6,7},{8,9},{9,10},{10,11},{12,13},{... | collective-permute-start | bytes 196616 | tf_op jit(solution)/shard_map/ppermute | solution.py:297
  21.0 5.7 %copy-start.10 = (f32[64,256]{1,0:T(8,128)}, f32[64,256]{1,0:T(8,128)S(1)}, u32[]{:S(2)}) copy-start(f32[64,256]{1,0:T(8,128)S(1)} %collective-permute-done.4.low_ref) | copy-start | bytes 196612
  21.0 5.7 %copy-start = (f32[2,64,256]{2,1,0:T(8,128)}, f32[2,64,256]{2,1,0:T(8,128)S(1)}, u32[]{:S(2)}) copy-start(f32[2,64,256]{2,1,0:T(8,128)S(1)} %collective-permute-done.3.r3) | copy-start | bytes 393220
  21.0 5.7 %copy-start.1 = (f32[2,64,256]{2,1,0:T(8,128)}, f32[2,64,256]{2,1,0:T(8,128)S(1)}, u32[]{:S(2)}) copy-start(f32[2,64,256]{2,1,0:T(8,128)S(1)} %collective-permute-done.2.r2) | copy-start | bytes 393220
  22.9 3.8 %copy-start.2 = (f32[2,64,256]{2,1,0:T(8,128)}, f32[2,64,256]{2,1,0:T(8,128)S(1)}, u32[]{:S(2)}) copy-start(f32[2,64,256]{2,1,0:T(8,128)S(1)} %collective-permute-done.1.r1) | copy-start | bytes 393220
  26.7 0.7 copy-start.3
  59.0 10.8 %collective-permute-start.10 = (f32[64,256]{1,0:T(8,128)}, f32[64,256]{1,0:T(8,128)S(1)}, u32[]{:S(2)}, u32[]{:S(2)}) collective-permute-start(f32[64,256]{1,0:T(8,128)} %get-tuple-element.16), channel_id=1, source_target_pairs={{0,1},{1,2},{2,3},{4,5},{5,6},{6,7},{8,9},{9,10},{10,11},{12,13},{... | collective-permute-start | bytes 196616 | tf_op jit(solution)/shard_map/ppermute | solution.py:297
  60.7 13.8 %collective-permute-start.6 = (f32[2,64,256]{2,1,0:T(8,128)}, f32[2,64,256]{2,1,0:T(8,128)S(1)}, u32[]{:S(2)}, u32[]{:S(2)}) collective-permute-start(f32[2,64,256]{2,1,0:T(8,128)} %get-tuple-element.12), channel_id=1, source_target_pairs={{0,8},{4,12},{8,16},{12,20},{16,24},{20,28},{1,9},{5,13},{9,17},{1... | collective-permute-start | bytes 393224 | tf_op jit(solution)/shard_map/ppermute | solution.py:297
  64.3 10.3 %collective-permute-start.7 = (f32[2,64,256]{2,1,0:T(8,128)}, f32[2,64,256]{2,1,0:T(8,128)S(1)}, u32[]{:S(2)}, u32[]{:S(2)}) collective-permute-start(f32[2,64,256]{2,1,0:T(8,128)} %get-tuple-element.13), channel_id=1, source_target_pairs={{0,4},{4,8},{8,12},{12,16},{16,20},{20,24},{24,28},{1,5},{5,9},{9,... | collective-permute-start | bytes 393224 | tf_op jit(solution)/shard_map/ppermute | solution.py:297
  67.3 7.8 %collective-permute-start.8 = (f32[2,64,256]{2,1,0:T(8,128)}, f32[2,64,256]{2,1,0:T(8,128)S(1)}, u32[]{:S(2)}, u32[]{:S(2)}) collective-permute-start(f32[2,64,256]{2,1,0:T(8,128)} %get-tuple-element.14), channel_id=1, source_target_pairs={{4,0},{8,4},{12,8},{16,12},{20,16},{24,20},{28,24},{5,1},{9,5},{13... | collective-permute-start | bytes 393224 | tf_op jit(solution)/shard_map/ppermute | solution.py:297
  68.6 11.0 %collective-permute-start.9 = (f32[2,64,256]{2,1,0:T(8,128)}, f32[2,64,256]{2,1,0:T(8,128)S(1)}, u32[]{:S(2)}, u32[]{:S(2)}) collective-permute-start(f32[2,64,256]{2,1,0:T(8,128)} %get-tuple-element.15), channel_id=1, source_target_pairs={{8,0},{12,4},{16,8},{20,12},{24,16},{28,20},{9,1},{13,5},{17,9},{2... | collective-permute-start | bytes 393224 | tf_op jit(solution)/shard_map/ppermute | solution.py:297
  69.9 9.7 %copy-start.9 = (f32[64,256]{1,0:T(8,128)}, f32[64,256]{1,0:T(8,128)S(1)}, u32[]{:S(2)}) copy-start(f32[64,256]{1,0:T(8,128)S(1)} %collective-permute-done.10.f0) | copy-start | bytes 196612
  69.9 4.7 %collective-permute-start.11 = (f32[64,256]{1,0:T(8,128)}, f32[64,256]{1,0:T(8,128)S(1)}, u32[]{:S(2)}, u32[]{:S(2)}) collective-permute-start(f32[64,256]{1,0:T(8,128)} %get-tuple-element.17), channel_id=1, source_target_pairs={{1,0},{2,1},{3,2},{5,4},{6,5},{7,6},{9,8},{10,9},{11,10},{13,12},{... | collective-permute-start | bytes 196616 | tf_op jit(solution)/shard_map/ppermute | solution.py:297
  74.6 5.1 %copy-start.11 = (f32[64,256]{1,0:T(8,128)}, f32[64,256]{1,0:T(8,128)S(1)}, u32[]{:S(2)}) copy-start(f32[64,256]{1,0:T(8,128)S(1)} %collective-permute-done.11.f1) | copy-start | bytes 196612
  74.6 5.1 %copy-start.4 = (f32[2,64,256]{2,1,0:T(8,128)}, f32[2,64,256]{2,1,0:T(8,128)S(1)}, u32[]{:S(2)}) copy-start(f32[2,64,256]{2,1,0:T(8,128)S(1)} %collective-permute-done.6.r0) | copy-start | bytes 393220
  74.6 5.1 %copy-start.5 = (f32[2,64,256]{2,1,0:T(8,128)}, f32[2,64,256]{2,1,0:T(8,128)S(1)}, u32[]{:S(2)}) copy-start(f32[2,64,256]{2,1,0:T(8,128)S(1)} %collective-permute-done.7.r1) | copy-start | bytes 393220
  75.1 4.6 %copy-start.6 = (f32[2,64,256]{2,1,0:T(8,128)}, f32[2,64,256]{2,1,0:T(8,128)S(1)}, u32[]{:S(2)}) copy-start(f32[2,64,256]{2,1,0:T(8,128)S(1)} %collective-permute-done.8.r2) | copy-start | bytes 393220
  79.6 0.6 copy-start.7

commit v2 on v1

--- a/solution.py
+++ b/solution.py
@@ -1,5 +1,3 @@
-import functools
-
 import jax
 import jax.numpy as jnp
 import numpy as np
@@ -119,12 +117,11 @@
     return face_ref[0, 0, chunk - 8 : chunk - 7, :]
 
 
-def pack_stage(x_ref, index_ref, live_ref, face_ref, pay_ref):
-    rows = jnp.concatenate(halves(x_ref[...]), 0)
-    for chunk in range(10):
-        spot = one_hot(x_ref.shape[1], listed(index_ref, live_ref, face_ref, chunk))
-        both = dot(rows, spot)
-        pay_ref[chunk] = both[:64] + both[64:]
+def pack_stage(rows, chunk, index_ref, live_ref, face_ref, list_ref, pay_ref):
+    spot = one_hot(rows.shape[1], listed(index_ref, live_ref, face_ref, chunk))
+    list_ref[chunk] = spot
+    both = dot(rows, spot)
+    pay_ref[chunk] = both[:64] + both[64:]
 
 
 def links_stage(links_ref, lo_ref, hi_ref, valid_ref):
@@ -151,10 +148,17 @@
             ref[i, to, LO : 2 * LO] = out[at : at + size].astype(BF)
 
 
-def gather_stage(first, count, size, at, src_ref, lo_ref, hi_ref, hot_ref, g_ref):
+def hot_stage(lo_ref, hot_ref):
     def body(i, carry):
-        spot = one_hot(LO, lo_ref[first + i])
-        hot_ref[first + i] = spot
+        hot_ref[i] = one_hot(LO, lo_ref[i])
+        return carry
+
+    lax.fori_loop(0, 26, body, 0)
+
+
+def gather_stage(first, count, size, at, src_ref, hi_ref, hot_ref, g_ref):
+    def body(i, carry):
+        spot = hot_ref[first + i]
         columns = spot.shape[1]
         if size == 8:
             out = dot(src_ref[i].astype(BF), spot)
@@ -236,94 +240,153 @@
     return dot(put_ref[...], hi) + dot(put_ref[...], lo)
 
 
-def finish_stage(index_ref, live_ref, face_ref, sens, back_chunk):
-    total = jnp.zeros((128, sens.shape[1]), F32)
-    for chunk in range(10):
-        spot = one_hot(sens.shape[1], listed(index_ref, live_ref, face_ref, chunk))
-        total = total + dot_t(jnp.concatenate(halves(back_chunk(chunk)), 0), spot)
-    return sens + total[:64] + total[64:]
+class Moves:
+    def __init__(self, sign, src, dst, send_sem, recv_sem):
+        plane, depth = lax.axis_index("plane"), lax.axis_index("depth")
+        planes, depths = lax.axis_size("plane"), lax.axis_size("depth")
+        self.refs = (src, dst, send_sem, recv_sem)
+        self.all = []
+        for g, o in enumerate(OFFSETS):
+            to, got = plane + sign * o, plane - sign * o
+            self.all.append((2 * g, 2 * g, 2, (to, depth), inside(to, planes), inside(got, planes)))
+        for chunk, o in ((8, -1), (9, 1)):
+            to, got = depth + o, depth - o
+            self.all.append((chunk, 17 - chunk, 1, (plane, to), inside(to, depths), inside(got, depths)))
+
+    def copy(self, m):
+        src, dst, send_sem, recv_sem = self.refs
+        start, end, count, device, _, _ = self.all[m]
+        return pltpu.make_async_remote_copy(
+            src_ref=src.at[pl.ds(start, count)],
+            dst_ref=dst.at[pl.ds(end, count)],
+            send_sem=send_sem.at[m],
+            recv_sem=recv_sem.at[m],
+            device_id=device,
+            device_id_type=pl.DeviceIdType.MESH,
+        )
+
+    def clear(self):
+        dst = self.refs[1]
+        for _, end, count, _, _, gets in self.all:
+
+            @pl.when(jnp.logical_not(gets))
+            def _():
+                dst[end : end + count] = jnp.zeros((count, 64, LO), F32)
+
+    def start(self, m):
+        @pl.when(self.all[m][4])
+        def _():
+            self.copy(m).start()
+
+    def wait_recv(self, m):
+        @pl.when(self.all[m][5])
+        def _():
+            self.copy(m).wait_recv()
+
+    def wait_send(self):
+        for m in range(6):
+
+            @pl.when(self.all[m][4])
+            def _():
+                self.copy(m).wait_send()
+
+
+def inside(at, count):
+    return jnp.logical_and(at >= 0, at < count)
+
+
+def greet():
+    plane, depth = lax.axis_index("plane"), lax.axis_index("depth")
+    planes, depths = lax.axis_size("plane"), lax.axis_size("depth")
+    barrier = pltpu.get_barrier_semaphore()
+    near = [((plane + o, depth), inside(plane + o, planes)) for o in OFFSETS]
+    near += [((plane, depth + o), inside(depth + o, depths)) for o in (-1, 1)]
+    for device, there in near:
+
+        @pl.when(there)
+        def _():
+            pl.semaphore_signal(
+                barrier, inc=1, device_id=device, device_id_type=pl.DeviceIdType.MESH
+            )
+
+    def wait():
+        pl.semaphore_wait(barrier, sum(jnp.where(there, 1, 0) for _, there in near))
+
+    return wait
 
 
 def main_kernel(
-    x_ref, energy_ref, links_ref, r0, r1, r2, r3, low_ref, up_ref,
+    x_ref, energy_ref, links_ref, index_ref, live_ref, face_ref,
     pick_ref, conv_ref, back_ref, put_ref, sums_ref,
-    cond_ref, sens_ref, b0, b1, b2, b3, blow_ref, bup_ref,
+    cond_ref, sens_ref,
     lo_ref, hi_ref, valid_ref, lc, le, lf, hot_ref, g_ref, sc, se, sf, mid_ref, d_ref,
+    list_ref, pay, got, bpay, bgot, send_sem, recv_sem, bsend_sem, brecv_sem,
 ):
+    wait_all = greet()
+    out = Moves(1, pay, got, send_sem, recv_sem)
+    home = Moves(-1, bpay, bgot, bsend_sem, brecv_sem)
+    out.clear()
+    home.clear()
+    rows = jnp.concatenate(halves(x_ref[...]), 0)
+    ORDERED = (0, 3, 1, 2, 4, 5)
+    for n, m in enumerate(ORDERED):
+        start, _, count = out.all[m][:3]
+        for chunk in range(start, start + count):
+            pack_stage(rows, chunk, index_ref, live_ref, face_ref, list_ref, pay)
+        if n == 0:
+            wait_all()
+        out.start(m)
     links_stage(links_ref, lo_ref, hi_ref, valid_ref)
-    got = (r0, r1, r2, r3)
-    sent = (b0, b1, b2, b3)
-    for h in range(14):
-        if h < 4:
-            chunk = x_ref[:, h * LO : (h + 1) * LO]
-        elif h < 12:
-            chunk = got[(h - 4) // 2][h % 2]
-        else:
-            chunk = (low_ref if h == 12 else up_ref)[...]
-        pick_stage(chunk, h, pick_ref, lc, le, lf)
-    gather_stage(0, NC, 8, 0, lc, lo_ref, hi_ref, hot_ref, g_ref)
-    gather_stage(NC, NE, 16, E_AT, le, lo_ref, hi_ref, hot_ref, g_ref)
-    gather_stage(NC + NE, NF, 32, F_AT, lf, lo_ref, hi_ref, hot_ref, g_ref)
+    hot_stage(lo_ref, hot_ref)
+    for h in range(4):
+        pick_stage(x_ref[:, h * LO : (h + 1) * LO], h, pick_ref, lc, le, lf)
+    for m in ORDERED:
+        out.wait_recv(m)
+        _, end, count = out.all[m][:3]
+        for chunk in range(end, end + count):
+            pick_stage(got[chunk], 4 + chunk, pick_ref, lc, le, lf)
+    gather_stage(0, NC, 8, 0, lc, hi_ref, hot_ref, g_ref)
+    gather_stage(NC, NE, 16, E_AT, le, hi_ref, hot_ref, g_ref)
+    gather_stage(NC + NE, NF, 32, F_AT, lf, hi_ref, hot_ref, g_ref)
     g_ref[M_AT:, :] = x_ref[...]
     filter_stage(energy_ref, conv_ref, back_ref, sums_ref, valid_ref, g_ref, cond_ref, sc, se, sf, mid_ref)
-    chunks = list(range(14))
-    scatter_stage(0, NC, 8, 0, sc, hi_ref, hot_ref, d_ref, chunks)
-    scatter_stage(NC, NE, 16, E_AT, se, hi_ref, hot_ref, d_ref, chunks)
-    scatter_stage(NC + NE, NF, 32, F_AT, sf, hi_ref, hot_ref, d_ref, chunks)
-    for h in range(14):
-        part = put_stage(h, put_ref, d_ref)
-        if h < 4:
-            columns = slice(h * LO, (h + 1) * LO)
-            sens_ref[:, columns] = part + mid_ref[:, columns]
-        elif h < 12:
-            sent[(h - 4) // 2][h % 2] = part
+    for chunks in (list(range(4, 14)), list(range(4))):
+        scatter_stage(0, NC, 8, 0, sc, hi_ref, hot_ref, d_ref, chunks)
+        scatter_stage(NC, NE, 16, E_AT, se, hi_ref, hot_ref, d_ref, chunks)
+        scatter_stage(NC + NE, NF, 32, F_AT, sf, hi_ref, hot_ref, d_ref, chunks)
+        if chunks[0]:
+            for m in ORDERED:
+                start, _, count = home.all[m][:3]
+                for chunk in range(start, start + count):
+                    bpay[chunk] = put_stage(4 + chunk, put_ref, d_ref)
+                home.start(m)
         else:
-            (blow_ref if h == 12 else bup_ref)[...] = part
-
-
-def final_kernel(sens_ref, r0, r1, r2, r3, f0, f1, index_ref, live_ref, face_ref, out_ref):
-    got = (r0, r1, r2, r3)
-
-    def back_chunk(chunk):
-        if chunk < 8:
-            return got[chunk // 2][chunk % 2]
-        return (f0 if chunk == 8 else f1)[...]
-
-    out_ref[...] = finish_stage(index_ref, live_ref, face_ref, sens_ref[...], back_chunk)
-
-
-def moved(shard, axis, by):
-    count = lax.axis_size(axis)
-    return lax.ppermute(shard, axis, [(i, i + by) for i in range(count) if 0 <= i + by < count])
+            for h in chunks:
+                columns = slice(h * LO, (h + 1) * LO)
+                sens_ref[:, columns] = put_stage(h, put_ref, d_ref) + mid_ref[:, columns]
+    total = jnp.zeros((128, x_ref.shape[1]), F32)
+    for m in ORDERED:
+        home.wait_recv(m)
+        _, end, count = home.all[m][:3]
+        for chunk in range(end, end + count):
+            total = total + dot_t(jnp.concatenate(halves(bgot[chunk]), 0), list_ref[chunk])
+    sens_ref[...] = sens_ref[...] + total[:64] + total[64:]
+    out.wait_send()
+    home.wait_send()
 
 
 VM = pl.BlockSpec(memory_space=pltpu.VMEM)
 SM = pl.BlockSpec(memory_space=pltpu.SMEM)
-PARAMS = pltpu.CompilerParams(vmem_limit_bytes=56 * 1024 * 1024)
-
-
-def shape(*dims):
-    return jax.ShapeDtypeStruct(dims, F32)
 
 
 def on_device(density, energy, links, send_index, send_live, face_index):
     blocks = density.shape[1]
     consts = [jnp.asarray(c) for c in constants()]
-    pay = pl.pallas_call(
-        pack_stage,
-        out_shape=shape(10, 64, LO),
-        in_specs=[VM, VM, SM, VM],
-        out_specs=VM,
-        compiler_params=PARAMS,
-    )(density, send_index, send_live, face_index)
-    got = [moved(pay[2 * g : 2 * g + 2], "plane", o) for g, o in enumerate(OFFSETS)]
-    up = moved(pay[8], "depth", -1)
-    low = moved(pay[9], "depth", 1)
-    outs = pl.pallas_call(
+    return pl.pallas_call(
         main_kernel,
-        out_shape=[shape(64, blocks)] * 2 + [shape(2, 64, LO)] * 4 + [shape(64, LO)] * 2,
-        in_specs=[VM] * 14,
-        out_specs=[VM] * 8,
+        out_shape=[jax.ShapeDtypeStruct((64, blocks), F32)] * 2,
+        in_specs=[VM] * 4 + [SM] + [VM] * 6,
+        out_specs=[VM] * 2,
         scratch_shapes=[
             pltpu.VMEM((26, 1, blocks), jnp.int32),
             pltpu.VMEM((26, 1, blocks), jnp.int32),
@@ -338,21 +401,20 @@
             pltpu.VMEM((NF, 64, blocks), BF),
             pltpu.VMEM((64, blocks), F32),
             pltpu.VMEM((14, M_AT, LO), F32),
+            pltpu.VMEM((10, blocks, LO), BF),
+            pltpu.VMEM((10, 64, LO), F32),
+            pltpu.VMEM((10, 64, LO), F32),
+            pltpu.VMEM((10, 64, LO), F32),
+            pltpu.VMEM((10, 64, LO), F32),
+            pltpu.SemaphoreType.DMA((6,)),
+            pltpu.SemaphoreType.DMA((6,)),
+            pltpu.SemaphoreType.DMA((6,)),
+            pltpu.SemaphoreType.DMA((6,)),
         ],
-        compiler_params=PARAMS,
-    )(density, energy, links, *got, low, up, *consts)
-    cond, sens = outs[:2]
-    returned = [moved(outs[2 + g], "plane", -o) for g, o in enumerate(OFFSETS)]
-    face_1 = moved(outs[6], "depth", -1)
-    face_0 = moved(outs[7], "depth", 1)
-    sens = pl.pallas_call(
-        final_kernel,
-        out_shape=shape(64, blocks),
-        in_specs=[VM] * 8 + [SM, VM],
-        out_specs=VM,
-        compiler_params=PARAMS,
-    )(sens, *returned, face_0, face_1, send_index, send_live, face_index)
-    return cond, sens
+        compiler_params=pltpu.CompilerParams(
+            vmem_limit_bytes=58 * 1024 * 1024, collective_id=0, has_side_effects=True
+        ),
+    )(density, energy, links, send_index, send_live, face_index, *consts)
 
 
 def solution(mesh):

time: 84.8 us -> 52.1 us (0.61)
  the two profiles are of different devices: /device:TPU:0 before, /device:TPU:16 now
where the time goes in v2:
time: 52.1 us; the launch traced here: 51.9 us
  Pallas kernels  48.8 us (94%)
  local copies, waits for them, and re-layouts  2.42 us (5%)
  between operations  0.65 us (1%)
    pallas_call x1, Pallas kernels, on_device(): pl.pallas_call(main_kernel, out_shape=[jax.ShapeDtypeStruct((64, blocks),...  48.8 us
    unnamed x4, local copies, waits for them, and re-layouts  2.42 us

profile of v2, /device:TPU:16, one launch (start us, length us, event | category | flops | bytes accessed | tf_op | source)
XLA Modules:
  0.0 51.9 jit_solution(7464233839699867539)
XLA Ops:
  0.6 48.8 %shard_map.122 = (f32[64,1024]{1,0:T(8,128)}, f32[64,1024]{1,0:T(8,128)}) custom-call(f32[64,1024]{1,0:T(8,128)} %x_ref.1, f32[64,1024]{1,0:T(8,128)} %energy_ref.1, s32[27,1024]{1,0:T(8,128)} %links_ref.1, s32[1,1,4,512]{3,2,1,0:T(4,128)} %index_ref.1, s32[1,1,4]{2,1,0:T(1,128)} %live_ref.1, s32[1,1,2,256]{3,2,1,0:T(2,128)} %face_ref.1, ...), custom_call_target="tpu_custom_call" | custom-call | tf_op jit(solution)/shard_map/pallas_call | solution.py:385
  49.5 0.0 copy-start
  49.5 1.7 %copy.15 = f32[64,1024]{1,0:T(8,128)} copy(f32[64,1024]{1,0:T(8,128)} %get-tuple-element.4) | data formatting | bytes 524288
  51.2 0.0 copy-done
  51.2 0.7 %copy.16 = f32[64,1024]{1,0:T(8,128)} copy(f32[64,1024]{1,0:T(8,128)S(1)} %copy-done) | data formatting | bytes 524288
Async XLA Ops:
  49.5 1.7 %copy-start = (f32[64,1024]{1,0:T(8,128)S(1)}, f32[64,1024]{1,0:T(8,128)}, u32[]{:S(2)}) copy-start(f32[64,1024]{1,0:T(8,128)} %get-tuple-element.5) | copy-start | bytes 786436

commit v3 on v2

--- a/solution.py
+++ b/solution.py
@@ -12,6 +12,7 @@
 FLOOR = 0.001
 PENALTY = 3.0
 LO = 256
+UNROLL = {8: 8, 16: 4, 32: 2}
 BF = jnp.bfloat16
 F32 = jnp.float32
 
@@ -104,8 +105,10 @@
 
 
 def one_hot(rows, index):
-    at = lax.broadcasted_iota(jnp.int32, (rows, index.shape[1]), 0)
-    return jnp.where(at == index, 1.0, 0.0).astype(BF)
+    at = lax.broadcasted_iota(jnp.int32, (rows, index.shape[1]), 0).astype(jnp.int16)
+    index = jnp.broadcast_to(index, (16, index.shape[1])).astype(jnp.int16)
+    index = jnp.concatenate([index] * (rows // 16), 0)
+    return jnp.where(at == index, jnp.ones((), BF), jnp.zeros((), BF))
 
 
 def listed(index_ref, live_ref, face_ref, chunk):
@@ -117,11 +120,12 @@
     return face_ref[0, 0, chunk - 8 : chunk - 7, :]
 
 
-def pack_stage(rows, chunk, index_ref, live_ref, face_ref, list_ref, pay_ref):
-    spot = one_hot(rows.shape[1], listed(index_ref, live_ref, face_ref, chunk))
-    list_ref[chunk] = spot
-    both = dot(rows, spot)
-    pay_ref[chunk] = both[:64] + both[64:]
+def pack_stage(rows, chunks, index_ref, live_ref, face_ref, list_ref, pay_ref):
+    for chunk in chunks:
+        spot = one_hot(rows.shape[1], listed(index_ref, live_ref, face_ref, chunk))
+        list_ref[:, chunk * LO : (chunk + 1) * LO] = spot
+        both = dot(rows, spot)
+        pay_ref[chunk] = both[:64] + both[64:]
 
 
 def links_stage(links_ref, lo_ref, hi_ref, valid_ref):
@@ -153,7 +157,7 @@
         hot_ref[i] = one_hot(LO, lo_ref[i])
         return carry
 
-    lax.fori_loop(0, 26, body, 0)
+    lax.fori_loop(0, 26, body, 0, unroll=2)
 
 
 def gather_stage(first, count, size, at, src_ref, hi_ref, hot_ref, g_ref):
@@ -175,10 +179,10 @@
             g_ref[pl.ds(pl.multiple_of(at + size * i + 8 * r, 8), 8), :] = acc[r]
         return carry
 
-    lax.fori_loop(0, count, body, 0)
-
-
-def filter_stage(energy_ref, conv_ref, back_ref, sums_ref, valid_ref, g_ref, cond_ref, sc, se, sf, mid_ref):
+    lax.fori_loop(0, count, body, 0, unroll=UNROLL[size])
+
+
+def filter_stage(energy_ref, conv_ref, back_ref, sums_ref, valid_ref, g_ref, filtered_ref, sc, se, sf, mid_ref):
     g_hi, g_lo = halves(g_ref[...])
     conv = conv_ref[...]
     main = dot(conv, g_hi)
@@ -187,7 +191,7 @@
     hs = hs[:64] + hs[64:128] + hs[128:]
     filtered = total / hs
     square = filtered * filtered
-    cond_ref[...] = FLOOR + square * filtered * (1.0 - FLOOR)
+    filtered_ref[...] = filtered
     scaled = -PENALTY * (1.0 - FLOOR) * square * energy_ref[...] / hs
     s_hi, s_lo = halves(scaled)
     spread = dot(back_ref[...], jnp.concatenate([s_hi, s_lo, s_hi], 0))
@@ -216,11 +220,12 @@
                 pieces.append(jnp.where(hi == h, rows, 0.0))
             left = jnp.concatenate(pieces, 0).astype(BF)
         else:
-            hi = jnp.broadcast_to(hi_ref[first + i], (16, columns))
+            hi = jnp.broadcast_to(hi_ref[first + i], (16, columns)).astype(jnp.int16)
             for h in chunks:
-                here = jnp.where(hi == h, 1.0, 0.0).astype(BF)
+                here = hi == jnp.int16(h)
                 for r in range(size // 8):
-                    pieces.append(rows[16 * r : 16 * r + 16] * here)
+                    part = rows[16 * r : 16 * r + 16]
+                    pieces.append(jnp.where(here, part, jnp.zeros((), BF)))
             left = jnp.concatenate(pieces, 0)
         out = dot_t(left, spot)
         to = pl.ds(pl.multiple_of(at + size * i, 8), size)
@@ -232,7 +237,7 @@
                 d_ref[h, to, :] = out[row : row + size] + out[row + size : row + 2 * size]
         return carry
 
-    lax.fori_loop(0, count, body, 0)
+    lax.fori_loop(0, count, body, 0, unroll=UNROLL[size])
 
 
 def put_stage(h, put_ref, d_ref):
@@ -318,7 +323,7 @@
 def main_kernel(
     x_ref, energy_ref, links_ref, index_ref, live_ref, face_ref,
     pick_ref, conv_ref, back_ref, put_ref, sums_ref,
-    cond_ref, sens_ref,
+    filtered_ref, sens_ref, far_ref,
     lo_ref, hi_ref, valid_ref, lc, le, lf, hot_ref, g_ref, sc, se, sf, mid_ref, d_ref,
     list_ref, pay, got, bpay, bgot, send_sem, recv_sem, bsend_sem, brecv_sem,
 ):
@@ -331,8 +336,8 @@
     ORDERED = (0, 3, 1, 2, 4, 5)
     for n, m in enumerate(ORDERED):
         start, _, count = out.all[m][:3]
-        for chunk in range(start, start + count):
-            pack_stage(rows, chunk, index_ref, live_ref, face_ref, list_ref, pay)
+        chunks = range(start, start + count)
+        pack_stage(rows, chunks, index_ref, live_ref, face_ref, list_ref, pay)
         if n == 0:
             wait_all()
         out.start(m)
@@ -349,7 +354,7 @@
     gather_stage(NC, NE, 16, E_AT, le, hi_ref, hot_ref, g_ref)
     gather_stage(NC + NE, NF, 32, F_AT, lf, hi_ref, hot_ref, g_ref)
     g_ref[M_AT:, :] = x_ref[...]
-    filter_stage(energy_ref, conv_ref, back_ref, sums_ref, valid_ref, g_ref, cond_ref, sc, se, sf, mid_ref)
+    filter_stage(energy_ref, conv_ref, back_ref, sums_ref, valid_ref, g_ref, filtered_ref, sc, se, sf, mid_ref)
     for chunks in (list(range(4, 14)), list(range(4))):
         scatter_stage(0, NC, 8, 0, sc, hi_ref, hot_ref, d_ref, chunks)
         scatter_stage(NC, NE, 16, E_AT, se, hi_ref, hot_ref, d_ref, chunks)
@@ -365,12 +370,17 @@
                 columns = slice(h * LO, (h + 1) * LO)
                 sens_ref[:, columns] = put_stage(h, put_ref, d_ref) + mid_ref[:, columns]
     total = jnp.zeros((128, x_ref.shape[1]), F32)
-    for m in ORDERED:
-        home.wait_recv(m)
-        _, end, count = home.all[m][:3]
-        for chunk in range(end, end + count):
-            total = total + dot_t(jnp.concatenate(halves(bgot[chunk]), 0), list_ref[chunk])
-    sens_ref[...] = sens_ref[...] + total[:64] + total[64:]
+    for group in ((0,), (3,), (1,), (2,), (4, 5)):
+        parts = []
+        for m in group:
+            home.wait_recv(m)
+        start = min(home.all[m][1] for m in group)
+        for chunk in (start, start + 1):
+            parts.append(jnp.concatenate(halves(bgot[chunk]), 0))
+        total = total + dot_t(
+            jnp.concatenate(parts, 1), list_ref[:, start * LO : (start + 2) * LO]
+        )
+    far_ref[...] = total[:64] + total[64:]
     out.wait_send()
     home.wait_send()
 
@@ -382,11 +392,11 @@
 def on_device(density, energy, links, send_index, send_live, face_index):
     blocks = density.shape[1]
     consts = [jnp.asarray(c) for c in constants()]
-    return pl.pallas_call(
+    filtered, near, far = pl.pallas_call(
         main_kernel,
-        out_shape=[jax.ShapeDtypeStruct((64, blocks), F32)] * 2,
+        out_shape=[jax.ShapeDtypeStruct((64, blocks), F32)] * 3,
         in_specs=[VM] * 4 + [SM] + [VM] * 6,
-        out_specs=[VM] * 2,
+        out_specs=[VM] * 3,
         scratch_shapes=[
             pltpu.VMEM((26, 1, blocks), jnp.int32),
             pltpu.VMEM((26, 1, blocks), jnp.int32),
@@ -401,7 +411,7 @@
             pltpu.VMEM((NF, 64, blocks), BF),
             pltpu.VMEM((64, blocks), F32),
             pltpu.VMEM((14, M_AT, LO), F32),
-            pltpu.VMEM((10, blocks, LO), BF),
+            pltpu.VMEM((blocks, 10 * LO), BF),
             pltpu.VMEM((10, 64, LO), F32),
             pltpu.VMEM((10, 64, LO), F32),
             pltpu.VMEM((10, 64, LO), F32),
@@ -415,6 +425,8 @@
             vmem_limit_bytes=58 * 1024 * 1024, collective_id=0, has_side_effects=True
         ),
     )(density, energy, links, send_index, send_live, face_index, *consts)
+    conductivity = FLOOR + filtered * filtered * filtered * (1.0 - FLOOR)
+    return conductivity, near + far
 
 
 def solution(mesh):

time: 52.1 us -> 42.6 us (0.82)
  the two profiles are of different devices: /device:TPU:16 before, /device:TPU:0 now
where the time goes in v3:
time: 42.6 us; the launch traced here: 42.5 us
  Pallas kernels  39.3 us (92%)
  other arithmetic  2.48 us (6%)
  between operations  0.66 us (2%)
    pallas_call x1, Pallas kernels, on_device(): pl.pallas_call(main_kernel, out_shape=[jax.ShapeDtypeStruct((64, blocks),...  39.3 us
    add x1, other arithmetic, on_device(): conductivity = FLOOR + filtered * filtered * filtered * (1.0 - FLOOR)  1.75 us

profile of v3, /device:TPU:0, one launch (start us, length us, event | category | flops | bytes accessed | tf_op | source)
XLA Modules:
  0.0 42.5 jit_solution(8437580914770742728)
XLA Ops:
  0.6 39.3 %shard_map.122 = (f32[64,1024]{1,0:T(8,128)}, f32[64,1024]{1,0:T(8,128)}, f32[64,1024]{1,0:T(8,128)}) custom-call(f32[64,1024]{1,0:T(8,128)} %x_ref.1, f32[64,1024]{1,0:T(8,128)} %energy_ref.1, s32[27,1024]{1,0:T(8,128)} %links_ref.1, s32[1,1,4,512]{3,2,1,0:T(4,128)} %index_ref.1, s32[1,1,4]{2,1,0:T(1,128)} %live_ref.1, s32[1,1,2,256]{3,2,1,0:T(2,128)} %face_ref.1, ...), custom_call_target="tpu_custom_call" | custom-call | tf_op jit(solution)/shard_map/pallas_call | solution.py:395
  40.0 0.0 copy-start
  40.0 0.0 copy-start.1
  40.0 1.7 %fusion.1 = f32[64,1024]{1,0:T(8,128)} fusion(f32[64,1024]{1,0:T(8,128)} %get-tuple-element.5), kind=kLoop, calls=%fused_computation.2 | loop fusion | flops 262144 | bytes 524288 | tf_op jit(solution)/shard_map/add | solution.py:428
  41.7 0.0 copy-done
  41.7 0.0 copy-done.1
  41.7 0.7 %add.11 = f32[64,1024]{1,0:T(8,128)} add(f32[64,1024]{1,0:T(8,128)S(1)} %copy-done, f32[64,1024]{1,0:T(8,128)S(1)} %copy-done.1) | non-fusion elementwise | flops 65536 | bytes 786432 | tf_op jit(solution)/shard_map/add | solution.py:429
Async XLA Ops:
  40.0 1.8 %copy-start = (f32[64,1024]{1,0:T(8,128)S(1)}, f32[64,1024]{1,0:T(8,128)}, u32[]{:S(2)}) copy-start(f32[64,1024]{1,0:T(8,128)} %get-tuple-element.6) | copy-start | bytes 786436
  40.0 1.8 %copy-start.1 = (f32[64,1024]{1,0:T(8,128)S(1)}, f32[64,1024]{1,0:T(8,128)}, u32[]{:S(2)}) copy-start(f32[64,1024]{1,0:T(8,128)} %get-tuple-element.7) | copy-start | bytes 786436

commit v4 on v3

--- a/solution.py
+++ b/solution.py
@@ -12,7 +12,7 @@
 FLOOR = 0.001
 PENALTY = 3.0
 LO = 256
-UNROLL = {8: 8, 16: 4, 32: 2}
+UNROLL = {8: 8, 16: 6, 32: 3}
 BF = jnp.bfloat16
 F32 = jnp.float32
 
@@ -160,23 +160,29 @@
     lax.fori_loop(0, 26, body, 0, unroll=2)
 
 
-def gather_stage(first, count, size, at, src_ref, hi_ref, hot_ref, g_ref):
+def gather_stage(first, count, size, at, src_ref, hi_ref, hot_ref, g_ref, chunks):
+    begin, end = chunks[0] * size, (chunks[-1] + 1) * size
+
     def body(i, carry):
         spot = hot_ref[first + i]
         columns = spot.shape[1]
         if size == 8:
-            out = dot(src_ref[i].astype(BF), spot)
+            out = dot(src_ref[i, begin:end].astype(BF), spot)
         else:
-            out = dot(src_ref[i], jnp.concatenate([spot, spot], 0))
+            out = dot(src_ref[i, begin:end], jnp.concatenate([spot, spot], 0))
         hi = jnp.broadcast_to(hi_ref[first + i], (8, columns))
-        acc = [jnp.zeros((8, columns), F32) for _ in range(size // 8)]
-        for h in range(14):
+        places = [pl.ds(pl.multiple_of(at + size * i + 8 * r, 8), 8) for r in range(size // 8)]
+        if chunks[0]:
+            acc = [g_ref[place, :] for place in places]
+        else:
+            acc = [jnp.zeros((8, columns), F32) for _ in places]
+        for n, h in enumerate(chunks):
             here = hi == h
             for r in range(size // 8):
-                row = h * size + r * 8
+                row = n * size + r * 8
                 acc[r] = jnp.where(here, out[row : row + 8], acc[r])
-        for r in range(size // 8):
-            g_ref[pl.ds(pl.multiple_of(at + size * i + 8 * r, 8), 8), :] = acc[r]
+        for place, value in zip(places, acc):
+            g_ref[place, :] = value
         return carry
 
     lax.fori_loop(0, count, body, 0, unroll=UNROLL[size])
@@ -327,6 +333,16 @@
     lo_ref, hi_ref, valid_ref, lc, le, lf, hot_ref, g_ref, sc, se, sf, mid_ref, d_ref,
     list_ref, pay, got, bpay, bgot, send_sem, recv_sem, bsend_sem, brecv_sem,
 ):
+    def gather_all(chunks):
+        gather_stage(0, NC, 8, 0, lc, hi_ref, hot_ref, g_ref, chunks)
+        gather_stage(NC, NE, 16, E_AT, le, hi_ref, hot_ref, g_ref, chunks)
+        gather_stage(NC + NE, NF, 32, F_AT, lf, hi_ref, hot_ref, g_ref, chunks)
+
+    def scatter_all(chunks):
+        scatter_stage(0, NC, 8, 0, sc, hi_ref, hot_ref, d_ref, chunks)
+        scatter_stage(NC, NE, 16, E_AT, se, hi_ref, hot_ref, d_ref, chunks)
+        scatter_stage(NC + NE, NF, 32, F_AT, sf, hi_ref, hot_ref, d_ref, chunks)
+
     wait_all = greet()
     out = Moves(1, pay, got, send_sem, recv_sem)
     home = Moves(-1, bpay, bgot, bsend_sem, brecv_sem)
@@ -345,30 +361,26 @@
     hot_stage(lo_ref, hot_ref)
     for h in range(4):
         pick_stage(x_ref[:, h * LO : (h + 1) * LO], h, pick_ref, lc, le, lf)
+    gather_all(range(4))
     for m in ORDERED:
         out.wait_recv(m)
         _, end, count = out.all[m][:3]
         for chunk in range(end, end + count):
             pick_stage(got[chunk], 4 + chunk, pick_ref, lc, le, lf)
-    gather_stage(0, NC, 8, 0, lc, hi_ref, hot_ref, g_ref)
-    gather_stage(NC, NE, 16, E_AT, le, hi_ref, hot_ref, g_ref)
-    gather_stage(NC + NE, NF, 32, F_AT, lf, hi_ref, hot_ref, g_ref)
+    gather_all(range(4, 14))
     g_ref[M_AT:, :] = x_ref[...]
     filter_stage(energy_ref, conv_ref, back_ref, sums_ref, valid_ref, g_ref, filtered_ref, sc, se, sf, mid_ref)
-    for chunks in (list(range(4, 14)), list(range(4))):
-        scatter_stage(0, NC, 8, 0, sc, hi_ref, hot_ref, d_ref, chunks)
-        scatter_stage(NC, NE, 16, E_AT, se, hi_ref, hot_ref, d_ref, chunks)
-        scatter_stage(NC + NE, NF, 32, F_AT, sf, hi_ref, hot_ref, d_ref, chunks)
-        if chunks[0]:
-            for m in ORDERED:
-                start, _, count = home.all[m][:3]
-                for chunk in range(start, start + count):
-                    bpay[chunk] = put_stage(4 + chunk, put_ref, d_ref)
-                home.start(m)
-        else:
-            for h in chunks:
-                columns = slice(h * LO, (h + 1) * LO)
-                sens_ref[:, columns] = put_stage(h, put_ref, d_ref) + mid_ref[:, columns]
+    for group in ((0, 3), (1, 2, 4, 5)):
+        spans = [home.all[m][0::2][:2] for m in group]
+        scatter_all([4 + chunk for start, count in spans for chunk in range(start, start + count)])
+        for m, (start, count) in zip(group, spans):
+            for chunk in range(start, start + count):
+                bpay[chunk] = put_stage(4 + chunk, put_ref, d_ref)
+            home.start(m)
+    scatter_all(range(4))
+    for h in range(4):
+        columns = slice(h * LO, (h + 1) * LO)
+        sens_ref[:, columns] = put_stage(h, put_ref, d_ref) + mid_ref[:, columns]
     total = jnp.zeros((128, x_ref.shape[1]), F32)
     for group in ((0,), (3,), (1,), (2,), (4, 5)):
         parts = []
@@ -422,7 +434,7 @@
             pltpu.SemaphoreType.DMA((6,)),
         ],
         compiler_params=pltpu.CompilerParams(
-            vmem_limit_bytes=58 * 1024 * 1024, collective_id=0, has_side_effects=True
+            vmem_limit_bytes=50 * 1024 * 1024, collective_id=0, has_side_effects=True
         ),
     )(density, energy, links, send_index, send_live, face_index, *consts)
     conductivity = FLOOR + filtered * filtered * filtered * (1.0 - FLOOR)

time: 42.6 us -> 51.2 us (1.20)
  local copies, waits for them, and re-layouts: 0.01 us -> 9.25 us
  other arithmetic: 2.48 us -> 1.47 us
    unnamed x4 -> x22, local copies, waits for them, and re-layouts: 0.01 us -> 9.25 us
    add x1, other arithmetic: 1.75 us -> 0.74 us  [on_device(): conductivity = FLOOR + filtered * filtered * filtered * (1.0 - FLOOR)]
where the time goes in v4:
time: 51.2 us; the launch traced here: 50.7 us
  Pallas kernels  39.3 us (77%)
  local copies, waits for them, and re-layouts  9.25 us (18%)
  other arithmetic  1.47 us (3%)
  between operations  0.66 us (1%)
    pallas_call x1, Pallas kernels, on_device(): pl.pallas_call(main_kernel, out_shape=[jax.ShapeDtypeStruct((64, blocks),...  39.3 us
    unnamed x22, local copies, waits for them, and re-layouts  9.25 us

profile of v4, /device:TPU:0, one launch (start us, length us, event | category | flops | bytes accessed | tf_op | source)
XLA Modules:
  0.0 50.7 jit_solution(6597753555181330359)
XLA Ops:
  0.6 0.0 copy-start
  0.6 0.9 %copy-done = f32[64,1024]{1,0:T(8,128)S(1)} copy-done((f32[64,1024]{1,0:T(8,128)S(1)}, f32[64,1024]{1,0:T(8,128)}, u32[]{:S(2)}) %copy-start) | copy-done | bytes 262168
  1.6 0.0 copy-start.1
  1.6 0.9 %copy-done.1 = f32[64,1024]{1,0:T(8,128)S(1)} copy-done((f32[64,1024]{1,0:T(8,128)S(1)}, f32[64,1024]{1,0:T(8,128)}, u32[]{:S(2)}) %copy-start.1) | copy-done | bytes 262168
  2.5 0.0 copy-start.2
  2.5 0.9 %copy-done.2 = bf16[512,192]{1,0:T(8,128)(2,1)S(1)} copy-done((bf16[512,192]{1,0:T(8,128)(2,1)S(1)}, bf16[512,192]{1,0:T(8,128)(2,1)}, u32[]{:S(2)}) %copy-start.2) | copy-done | bytes 196632
  3.5 0.0 copy-start.3
  3.5 0.9 %copy-done.3 = bf16[832,128]{1,0:T(8,128)(2,1)S(1)} copy-done((bf16[832,128]{1,0:T(8,128)(2,1)S(1)}, bf16[832,128]{1,0:T(8,128)(2,1)}, u32[]{:S(2)}) %copy-start.3) | copy-done | bytes 213016
  4.4 0.0 copy-start.4
  4.4 0.9 %copy-done.4 = s32[27,1024]{1,0:T(8,128)S(1)} copy-done((s32[27,1024]{1,0:T(8,128)S(1)}, s32[27,1024]{1,0:T(8,128)}, u32[]{:S(2)}) %copy-start.4) | copy-done | bytes 110616
  5.3 0.0 copy-start.5
  5.3 0.9 %copy-done.5 = bf16[128,512]{1,0:T(8,128)(2,1)S(1)} copy-done((bf16[128,512]{1,0:T(8,128)(2,1)S(1)}, bf16[128,512]{1,0:T(8,128)(2,1)}, u32[]{:S(2)}) %copy-start.5) | copy-done | bytes 131096
  6.2 0.0 copy-start.6
  6.2 0.8 %copy-done.6 = bf16[64,448]{1,0:T(8,128)(2,1)S(1)} copy-done((bf16[64,448]{1,0:T(8,128)(2,1)S(1)}, bf16[64,448]{1,0:T(8,128)(2,1)}, u32[]{:S(2)}) %copy-start.6) | copy-done | bytes 57368
  7.1 0.0 copy-start.7
  7.1 0.8 %copy-done.7 = bf16[192,32]{1,0:T(8,128)(2,1)S(1)} copy-done((bf16[192,32]{1,0:T(8,128)(2,1)S(1)}, bf16[192,32]{1,0:T(8,128)(2,1)}, u32[]{:S(2)}) %copy-start.7) | copy-done | bytes 12312
  7.9 0.0 copy-start.8
  7.9 0.7 %copy-done.8 = s32[1,1,4,512]{3,2,1,0:T(4,128)S(1)} copy-done((s32[1,1,4,512]{3,2,1,0:T(4,128)S(1)}, s32[1,1,4,512]{3,2,1,0:T(4,128)}, u32[]{:S(2)}) %copy-start.8) | copy-done | bytes 8216
  8.6 0.0 copy-start.9
  8.6 0.7 %copy-done.9 = s32[1,1,2,256]{3,2,1,0:T(2,128)S(1)} copy-done((s32[1,1,2,256]{3,2,1,0:T(2,128)S(1)}, s32[1,1,2,256]{3,2,1,0:T(2,128)}, u32[]{:S(2)}) %copy-start.9) | copy-done | bytes 2072
  9.2 0.0 copy-start.10
  9.2 0.7 %copy-done.10 = s32[1,1,4]{2,1,0:T(1,128)S(1)} copy-done((s32[1,1,4]{2,1,0:T(1,128)S(1)}, s32[1,1,4]{2,1,0:T(1,128)}, u32[]{:S(2)}) %copy-start.10) | copy-done | bytes 40
  9.9 39.3 %shard_map.122 = (f32[64,1024]{1,0:T(8,128)S(1)}, f32[64,1024]{1,0:T(8,128)S(1)}, f32[64,1024]{1,0:T(8,128)S(1)}) custom-call(f32[64,1024]{1,0:T(8,128)S(1)} %copy-done, f32[64,1024]{1,0:T(8,128)S(1)} %copy-done.1, s32[27,1024]{1,0:T(8,128)S(1)} %copy-done.4, s32[1,1,4,512]{3,2,1,0:T(4,128)S(1)} %copy-done.8, s32[1,1,4]{2,1,0:T(1,128)S(1)} %copy-done.10, ...), custom_call_target="tpu_custom_call" | custom-call | tf_op jit(solution)/shard_map/pallas_call | solution.py:407
  49.2 0.7 %fusion.1 = f32[64,1024]{1,0:T(8,128)} fusion(f32[64,1024]{1,0:T(8,128)S(1)} %get-tuple-element.5), kind=kLoop, calls=%fused_computation.2 | loop fusion | flops 262144 | bytes 524288 | tf_op jit(solution)/shard_map/add | solution.py:440
  50.0 0.7 %add.11 = f32[64,1024]{1,0:T(8,128)} add(f32[64,1024]{1,0:T(8,128)S(1)} %get-tuple-element.6, f32[64,1024]{1,0:T(8,128)S(1)} %get-tuple-element.7) | non-fusion elementwise | flops 65536 | bytes 786432 | tf_op jit(solution)/shard_map/add | solution.py:441
Async XLA Ops:
  0.6 1.0 %copy-start = (f32[64,1024]{1,0:T(8,128)S(1)}, f32[64,1024]{1,0:T(8,128)}, u32[]{:S(2)}) copy-start(f32[64,1024]{1,0:T(8,128)} %x_ref.1) | copy-start | bytes 786436
  1.6 0.9 %copy-start.1 = (f32[64,1024]{1,0:T(8,128)S(1)}, f32[64,1024]{1,0:T(8,128)}, u32[]{:S(2)}) copy-start(f32[64,1024]{1,0:T(8,128)} %energy_ref.1) | copy-start | bytes 786436
  2.5 0.9 %copy-start.2 = (bf16[512,192]{1,0:T(8,128)(2,1)S(1)}, bf16[512,192]{1,0:T(8,128)(2,1)}, u32[]{:S(2)}) copy-start(bf16[512,192]{1,0:T(8,128)(2,1)} %constant.16.clone.back_ref) | copy-start | bytes 589828
  3.5 0.9 %copy-start.3 = (bf16[832,128]{1,0:T(8,128)(2,1)S(1)}, bf16[832,128]{1,0:T(8,128)(2,1)}, u32[]{:S(2)}) copy-start(bf16[832,128]{1,0:T(8,128)(2,1)} %constant.14.clone.pick_ref) | copy-start | bytes 638980
  4.4 0.9 %copy-start.4 = (s32[27,1024]{1,0:T(8,128)S(1)}, s32[27,1024]{1,0:T(8,128)}, u32[]{:S(2)}) copy-start(s32[27,1024]{1,0:T(8,128)} %links_ref.1) | copy-start | bytes 331780
  5.3 0.9 %copy-start.5 = (bf16[128,512]{1,0:T(8,128)(2,1)S(1)}, bf16[128,512]{1,0:T(8,128)(2,1)}, u32[]{:S(2)}) copy-start(bf16[128,512]{1,0:T(8,128)(2,1)} %constant.15.clone.conv_ref) | copy-start | bytes 393220
  6.2 0.8 %copy-start.6 = (bf16[64,448]{1,0:T(8,128)(2,1)S(1)}, bf16[64,448]{1,0:T(8,128)(2,1)}, u32[]{:S(2)}) copy-start(bf16[64,448]{1,0:T(8,128)(2,1)} %constant.17.clone.put_ref) | copy-start | bytes 172036
  7.1 0.8 %copy-start.7 = (bf16[192,32]{1,0:T(8,128)(2,1)S(1)}, bf16[192,32]{1,0:T(8,128)(2,1)}, u32[]{:S(2)}) copy-start(bf16[192,32]{1,0:T(8,128)(2,1)} %constant.18.clone.sums_ref) | copy-start | bytes 36868
  7.9 0.7 %copy-start.8 = (s32[1,1,4,512]{3,2,1,0:T(4,128)S(1)}, s32[1,1,4,512]{3,2,1,0:T(4,128)}, u32[]{:S(2)}) copy-start(s32[1,1,4,512]{3,2,1,0:T(4,128)} %index_ref.1) | copy-start | bytes 24580
  8.6 0.7 %copy-start.9 = (s32[1,1,2,256]{3,2,1,0:T(2,128)S(1)}, s32[1,1,2,256]{3,2,1,0:T(2,128)}, u32[]{:S(2)}) copy-start(s32[1,1,2,256]{3,2,1,0:T(2,128)} %face_ref.1) | copy-start | bytes 6148
  9.2 0.7 %copy-start.10 = (s32[1,1,4]{2,1,0:T(1,128)S(1)}, s32[1,1,4]{2,1,0:T(1,128)}, u32[]{:S(2)}) copy-start(s32[1,1,4]{2,1,0:T(1,128)} %live_ref.1) | copy-start | bytes 52

commit v5 on v3

--- a/solution.py
+++ b/solution.py
@@ -48,34 +48,35 @@
 E_AT, F_AT = C_ROWS, C_ROWS + E_ROWS
 M_AT = F_AT + F_ROWS
 ALL_ROWS = M_AT + 64
+G_ROWS = 4 * NC + E_ROWS + F_ROWS
+PAIRS = NC // 2
+SETS = PAIRS + NE + NF
+LANES = 128
 
 
 def constants():
-    pick = np.zeros((C_ROWS + 2 * E_ROWS + 2 * F_ROWS, 128), np.float32)
+    pick = np.zeros((G_ROWS, 128), np.float32)
     conv = np.zeros((64, ALL_ROWS), np.float32)
     back = np.zeros((ALL_ROWS, 64), np.float32)
     put = np.zeros((64, M_AT), np.float32)
+    row = 0
+    for k in ORDER:
+        for j in USED[k]:
+            pick[row, j] = pick[row, 64 + j] = 1
+            conv[:, row] = W[k][:, j]
+            row += 1
+    conv[:, G_ROWS : G_ROWS + 64] = W[13]
     for i, k in enumerate(CORNERS):
         for r, j in enumerate(USED[k]):
-            pick[8 * i + r, j] = 1
-            pick[8 * i + 4 + r, 64 + j] = 1
             for row in (8 * i + r, 8 * i + 4 + r):
-                conv[:, row] = W[k][:, j]
                 back[row] = W[k][:, j]
                 put[j, row] = 1
-    for kinds, size, at, src in (
-        (EDGES, 16, E_AT, C_ROWS),
-        (FACES, 32, F_AT, C_ROWS + 2 * E_ROWS),
-    ):
+    for kinds, size, at in ((EDGES, 16, E_AT), (FACES, 32, F_AT)):
         for i, k in enumerate(kinds):
             for r, j in enumerate(USED[k]):
-                pick[src + size * i + r, j] = 1
-                pick[src + size * len(kinds) + size * i + r, 64 + j] = 1
                 row = at + size * i + r
-                conv[:, row] = W[k][:, j]
                 back[row] = W[k][:, j]
                 put[j, row] = 1
-    conv[:, M_AT:] = W[13]
     back[M_AT:] = W[13].T
     sums = np.zeros((64, 32), np.float32)
     for i, k in enumerate(ORDER + [13]):
@@ -128,28 +129,34 @@
         pay_ref[chunk] = both[:64] + both[64:]
 
 
-def links_stage(links_ref, lo_ref, hi_ref, valid_ref):
+def links_stage(links_ref, lo_ref, hi_ref, valid_ref, lane_ref, part_ref):
     columns = links_ref.shape[1]
     for i, k in enumerate(ORDER):
         row = links_ref[k : k + 1, :]
         lo_ref[i] = row & (LO - 1)
         hi_ref[i] = row >> 8
         valid_ref[i : i + 1, :] = jnp.where(row != 14 * LO, 1.0, 0.0)
+    upper = lax.broadcasted_iota(jnp.int32, (8, columns), 0) < 4
+    for i in range(SETS):
+        if i < PAIRS:
+            first, second = (links_ref[k : k + 1, :] for k in CORNERS[2 * i : 2 * i + 2])
+            link = jnp.where(
+                upper, jnp.broadcast_to(first, (8, columns)), jnp.broadcast_to(second, (8, columns))
+            )
+        else:
+            k = ORDER[i + PAIRS]
+            link = jnp.broadcast_to(links_ref[k : k + 1, :], (8, columns))
+        lane_ref[i] = link & (LANES - 1)
+        part_ref[i] = link >> 7
     valid_ref[26:27, :] = jnp.ones((1, columns), F32)
     valid_ref[27:32, :] = jnp.zeros((5, columns), F32)
 
 
-def pick_stage(chunk, h, pick_ref, lc, le, lf):
+def pick_stage(chunk, h, pick_ref, src_ref):
     out = dot(pick_ref[...], jnp.concatenate(halves(chunk), 0))
-    for i in range(NC):
-        lc[i, pl.ds(pl.multiple_of(h * 8, 8), 8), :] = out[8 * i : 8 * i + 8]
-    for src, size, count, ref in ((C_ROWS, 16, NE, le), (C_ROWS + 2 * E_ROWS, 32, NF, lf)):
-        to = pl.ds(pl.multiple_of(h * size, size), size)
-        for i in range(count):
-            at = src + size * i
-            ref[i, to, 0:LO] = out[at : at + size].astype(BF)
-            at = at + size * count
-            ref[i, to, LO : 2 * LO] = out[at : at + size].astype(BF)
+    for half in range(2):
+        part = out[:, half * LANES : (half + 1) * LANES]
+        src_ref[:, 2 * h + half] = part.reshape(G_ROWS // 8, 8, LANES)
 
 
 def hot_stage(lo_ref, hot_ref):
@@ -160,26 +167,51 @@
     lax.fori_loop(0, 26, body, 0, unroll=2)
 
 
-def gather_stage(first, count, size, at, src_ref, hi_ref, hot_ref, g_ref):
+ALONG = lax.GatherDimensionNumbers(
+    offset_dims=(),
+    collapsed_slice_dims=(1,),
+    start_index_map=(1,),
+    operand_batching_dims=(0,),
+    start_indices_batching_dims=(0,),
+)
+
+
+def along(table, index):
+    return lax.gather(
+        table,
+        index[..., None],
+        ALONG,
+        (1, 1),
+        mode=lax.GatherScatterMode.PROMISE_IN_BOUNDS,
+    )
+
+
+def gather_stage(first, count, groups, at, src_ref, lane_ref, part_ref, g_ref, parts):
+    columns = lane_ref.shape[2]
+    step = 4 * LANES
+
     def body(i, carry):
-        spot = hot_ref[first + i]
-        columns = spot.shape[1]
-        if size == 8:
-            out = dot(src_ref[i].astype(BF), spot)
-        else:
-            out = dot(src_ref[i], jnp.concatenate([spot, spot], 0))
-        hi = jnp.broadcast_to(hi_ref[first + i], (8, columns))
-        acc = [jnp.zeros((8, columns), F32) for _ in range(size // 8)]
-        for h in range(14):
-            here = hi == h
-            for r in range(size // 8):
-                row = h * size + r * 8
-                acc[r] = jnp.where(here, out[row : row + 8], acc[r])
-        for r in range(size // 8):
-            g_ref[pl.ds(pl.multiple_of(at + size * i + 8 * r, 8), 8), :] = acc[r]
+        for begin in range(0, columns, step):
+            spans = [slice(c, c + LANES) for c in range(begin, begin + step, LANES)]
+            lane = [lane_ref[first + i, :, span] for span in spans]
+            part = [part_ref[first + i, :, span] for span in spans]
+            rows = [pl.ds(pl.multiple_of(8 * (at + groups * i + q), 8), 8) for q in range(groups)]
+            if parts[0]:
+                acc = [[g_ref[row, span] for span in spans] for row in rows]
+            else:
+                acc = [[jnp.zeros((8, LANES), F32) for _ in spans] for _ in rows]
+            for h in parts:
+                here = [p == h for p in part]
+                for q in range(groups):
+                    table = src_ref[at + groups * i + q, h]
+                    for t in range(len(spans)):
+                        acc[q][t] = jnp.where(here[t], along(table, lane[t]), acc[q][t])
+            for q in range(groups):
+                for t, span in enumerate(spans):
+                    g_ref[rows[q], span] = acc[q][t]
         return carry
 
-    lax.fori_loop(0, count, body, 0, unroll=UNROLL[size])
+    lax.fori_loop(0, count, body, 0)
 
 
 def filter_stage(energy_ref, conv_ref, back_ref, sums_ref, valid_ref, g_ref, filtered_ref, sc, se, sf, mid_ref):
@@ -324,9 +356,15 @@
     x_ref, energy_ref, links_ref, index_ref, live_ref, face_ref,
     pick_ref, conv_ref, back_ref, put_ref, sums_ref,
     filtered_ref, sens_ref, far_ref,
-    lo_ref, hi_ref, valid_ref, lc, le, lf, hot_ref, g_ref, sc, se, sf, mid_ref, d_ref,
+    lo_ref, hi_ref, valid_ref, lane_ref, part_ref, src_ref, hot_ref, g_ref, sc, se, sf, mid_ref, d_ref,
     list_ref, pay, got, bpay, bgot, send_sem, recv_sem, bsend_sem, brecv_sem,
 ):
+    def gather_all(parts):
+        refs = (src_ref, lane_ref, part_ref, g_ref, parts)
+        gather_stage(0, PAIRS, 1, 0, *refs)
+        gather_stage(PAIRS, NE, 2, PAIRS, *refs)
+        gather_stage(PAIRS + NE, NF, 4, PAIRS + 2 * NE, *refs)
+
     wait_all = greet()
     out = Moves(1, pay, got, send_sem, recv_sem)
     home = Moves(-1, bpay, bgot, bsend_sem, brecv_sem)
@@ -341,19 +379,19 @@
         if n == 0:
             wait_all()
         out.start(m)
-    links_stage(links_ref, lo_ref, hi_ref, valid_ref)
+    links_stage(links_ref, lo_ref, hi_ref, valid_ref, lane_ref, part_ref)
+    for h in range(4):
+        pick_stage(x_ref[:, h * LO : (h + 1) * LO], h, pick_ref, src_ref)
+    g_ref[G_ROWS : G_ROWS + 64, :] = x_ref[...]
+    g_ref[G_ROWS + 64 :, :] = jnp.zeros((ALL_ROWS - G_ROWS - 64, x_ref.shape[1]), F32)
     hot_stage(lo_ref, hot_ref)
-    for h in range(4):
-        pick_stage(x_ref[:, h * LO : (h + 1) * LO], h, pick_ref, lc, le, lf)
+    gather_all(range(8))
     for m in ORDERED:
         out.wait_recv(m)
         _, end, count = out.all[m][:3]
         for chunk in range(end, end + count):
-            pick_stage(got[chunk], 4 + chunk, pick_ref, lc, le, lf)
-    gather_stage(0, NC, 8, 0, lc, hi_ref, hot_ref, g_ref)
-    gather_stage(NC, NE, 16, E_AT, le, hi_ref, hot_ref, g_ref)
-    gather_stage(NC + NE, NF, 32, F_AT, lf, hi_ref, hot_ref, g_ref)
-    g_ref[M_AT:, :] = x_ref[...]
+            pick_stage(got[chunk], 4 + chunk, pick_ref, src_ref)
+    gather_all(range(8, 28))
     filter_stage(energy_ref, conv_ref, back_ref, sums_ref, valid_ref, g_ref, filtered_ref, sc, se, sf, mid_ref)
     for chunks in (list(range(4, 14)), list(range(4))):
         scatter_stage(0, NC, 8, 0, sc, hi_ref, hot_ref, d_ref, chunks)
@@ -401,9 +439,9 @@
             pltpu.VMEM((26, 1, blocks), jnp.int32),
             pltpu.VMEM((26, 1, blocks), jnp.int32),
             pltpu.VMEM((32, blocks), F32),
-            pltpu.VMEM((NC, 14 * 8, LO), F32),
-            pltpu.VMEM((NE, 14 * 16, 2 * LO), BF),
-            pltpu.VMEM((NF, 14 * 32, 2 * LO), BF),
+            pltpu.VMEM((SETS, 8, blocks), jnp.int32),
+            pltpu.VMEM((SETS, 8, blocks), jnp.int32),
+            pltpu.VMEM((G_ROWS // 8, 28, 8, LANES), F32),
             pltpu.VMEM((26, LO, blocks), BF),
             pltpu.VMEM((ALL_ROWS, blocks), F32),
             pltpu.VMEM((NC, 8, blocks), F32),

time: 42.6 us -> 66.9 us (1.57)
  Pallas kernels: 39.3 us -> 63.6 us
    pallas_call x1, Pallas kernels: 39.3 us -> 63.6 us  [on_device(): pl.pallas_call(main_kernel, out_shape=[jax.ShapeDtypeStruct((64, blocks),...]
where the time goes in v5:
time: 66.9 us; the launch traced here: 66.7 us
  Pallas kernels  63.6 us (95%)
  other arithmetic  2.48 us (4%)
    pallas_call x1, Pallas kernels, on_device(): pl.pallas_call(main_kernel, out_shape=[jax.ShapeDtypeStruct((64, blocks),...  63.6 us
    add x1, other arithmetic, on_device(): conductivity = FLOOR + filtered * filtered * filtered * (1.0 - FLOOR)  1.75 us

profile of v5, /device:TPU:0, one launch (start us, length us, event | category | flops | bytes accessed | tf_op | source)
XLA Modules:
  0.0 66.7 jit_solution(18336028906010923649)
XLA Ops:
  0.6 63.6 %shard_map.122 = (f32[64,1024]{1,0:T(8,128)}, f32[64,1024]{1,0:T(8,128)}, f32[64,1024]{1,0:T(8,128)}) custom-call(f32[64,1024]{1,0:T(8,128)} %x_ref.1, f32[64,1024]{1,0:T(8,128)} %energy_ref.1, s32[27,1024]{1,0:T(8,128)} %links_ref.1, s32[1,1,4,512]{3,2,1,0:T(4,128)} %index_ref.1, s32[1,1,4]{2,1,0:T(1,128)} %live_ref.1, s32[1,1,2,256]{3,2,1,0:T(2,128)} %face_ref.1, ...), custom_call_target="tpu_custom_call" | custom-call | tf_op jit(solution)/shard_map/pallas_call | solution.py:433
  64.2 0.0 copy-start
  64.3 0.0 copy-start.1
  64.3 1.7 %fusion.1 = f32[64,1024]{1,0:T(8,128)} fusion(f32[64,1024]{1,0:T(8,128)} %get-tuple-element.5), kind=kLoop, calls=%fused_computation.2 | loop fusion | flops 262144 | bytes 524288 | tf_op jit(solution)/shard_map/add | solution.py:466
  66.0 0.0 copy-done
  66.0 0.0 copy-done.1
  66.0 0.7 %add.11 = f32[64,1024]{1,0:T(8,128)} add(f32[64,1024]{1,0:T(8,128)S(1)} %copy-done, f32[64,1024]{1,0:T(8,128)S(1)} %copy-done.1) | non-fusion elementwise | flops 65536 | bytes 786432 | tf_op jit(solution)/shard_map/add | solution.py:467
Async XLA Ops:
  64.2 1.8 %copy-start = (f32[64,1024]{1,0:T(8,128)S(1)}, f32[64,1024]{1,0:T(8,128)}, u32[]{:S(2)}) copy-start(f32[64,1024]{1,0:T(8,128)} %get-tuple-element.6) | copy-start | bytes 786436
  64.3 1.8 %copy-start.1 = (f32[64,1024]{1,0:T(8,128)S(1)}, f32[64,1024]{1,0:T(8,128)}, u32[]{:S(2)}) copy-start(f32[64,1024]{1,0:T(8,128)} %get-tuple-element.7) | copy-start | bytes 786436

commit v6 on v3

--- a/solution.py
+++ b/solution.py
@@ -152,31 +152,33 @@
             ref[i, to, LO : 2 * LO] = out[at : at + size].astype(BF)
 
 
-def hot_stage(lo_ref, hot_ref):
+def gather_stage(first, count, size, at, src_ref, lo_ref, hi_ref, hot_ref, g_ref, chunks):
+    begin, end = chunks[0] * size, (chunks[-1] + 1) * size
+    columns = g_ref.shape[1]
+
     def body(i, carry):
-        hot_ref[i] = one_hot(LO, lo_ref[i])
-        return carry
-
-    lax.fori_loop(0, 26, body, 0, unroll=2)
-
-
-def gather_stage(first, count, size, at, src_ref, hi_ref, hot_ref, g_ref):
-    def body(i, carry):
-        spot = hot_ref[first + i]
-        columns = spot.shape[1]
+        places = [pl.ds(pl.multiple_of(at + size * i + 8 * r, 8), 8) for r in range(size // 8)]
+        left = src_ref[i, begin:end]
         if size == 8:
-            out = dot(src_ref[i].astype(BF), spot)
-        else:
-            out = dot(src_ref[i], jnp.concatenate([spot, spot], 0))
-        hi = jnp.broadcast_to(hi_ref[first + i], (8, columns))
-        acc = [jnp.zeros((8, columns), F32) for _ in range(size // 8)]
-        for h in range(14):
-            here = hi == h
-            for r in range(size // 8):
-                row = h * size + r * 8
-                acc[r] = jnp.where(here, out[row : row + 8], acc[r])
-        for r in range(size // 8):
-            g_ref[pl.ds(pl.multiple_of(at + size * i + 8 * r, 8), 8), :] = acc[r]
+            left = left.astype(BF)
+        for t in range(0, columns, LO):
+            span = slice(t, t + LO)
+            if chunks[0]:
+                spot = hot_ref[first + i, :, span]
+                acc = [g_ref[place, span] for place in places]
+            else:
+                spot = one_hot(LO, lo_ref[first + i, :, span])
+                hot_ref[first + i, :, span] = spot
+                acc = [jnp.zeros((8, LO), F32) for _ in places]
+            out = dot(left, spot if size == 8 else jnp.concatenate([spot, spot], 0))
+            hi = jnp.broadcast_to(hi_ref[first + i, :, span], (8, LO))
+            for n, h in enumerate(chunks):
+                here = hi == h
+                for r in range(size // 8):
+                    row = n * size + r * 8
+                    acc[r] = jnp.where(here, out[row : row + 8], acc[r])
+            for place, value in zip(places, acc):
+                g_ref[place, span] = value
         return carry
 
     lax.fori_loop(0, count, body, 0, unroll=UNROLL[size])
@@ -323,10 +325,16 @@
 def main_kernel(
     x_ref, energy_ref, links_ref, index_ref, live_ref, face_ref,
     pick_ref, conv_ref, back_ref, put_ref, sums_ref,
-    filtered_ref, sens_ref, far_ref,
+    result_ref,
     lo_ref, hi_ref, valid_ref, lc, le, lf, hot_ref, g_ref, sc, se, sf, mid_ref, d_ref,
     list_ref, pay, got, bpay, bgot, send_sem, recv_sem, bsend_sem, brecv_sem,
 ):
+    def gather_all(chunks):
+        refs = (lo_ref, hi_ref, hot_ref, g_ref, chunks)
+        gather_stage(0, NC, 8, 0, lc, *refs)
+        gather_stage(NC, NE, 16, E_AT, le, *refs)
+        gather_stage(NC + NE, NF, 32, F_AT, lf, *refs)
+
     wait_all = greet()
     out = Moves(1, pay, got, send_sem, recv_sem)
     home = Moves(-1, bpay, bgot, bsend_sem, brecv_sem)
@@ -342,19 +350,17 @@
             wait_all()
         out.start(m)
     links_stage(links_ref, lo_ref, hi_ref, valid_ref)
-    hot_stage(lo_ref, hot_ref)
     for h in range(4):
         pick_stage(x_ref[:, h * LO : (h + 1) * LO], h, pick_ref, lc, le, lf)
+    gather_all(range(4))
     for m in ORDERED:
         out.wait_recv(m)
         _, end, count = out.all[m][:3]
         for chunk in range(end, end + count):
             pick_stage(got[chunk], 4 + chunk, pick_ref, lc, le, lf)
-    gather_stage(0, NC, 8, 0, lc, hi_ref, hot_ref, g_ref)
-    gather_stage(NC, NE, 16, E_AT, le, hi_ref, hot_ref, g_ref)
-    gather_stage(NC + NE, NF, 32, F_AT, lf, hi_ref, hot_ref, g_ref)
+    gather_all(range(4, 14))
     g_ref[M_AT:, :] = x_ref[...]
-    filter_stage(energy_ref, conv_ref, back_ref, sums_ref, valid_ref, g_ref, filtered_ref, sc, se, sf, mid_ref)
+    filter_stage(energy_ref, conv_ref, back_ref, sums_ref, valid_ref, g_ref, result_ref.at[0:64], sc, se, sf, mid_ref)
     for chunks in (list(range(4, 14)), list(range(4))):
         scatter_stage(0, NC, 8, 0, sc, hi_ref, hot_ref, d_ref, chunks)
         scatter_stage(NC, NE, 16, E_AT, se, hi_ref, hot_ref, d_ref, chunks)
@@ -368,7 +374,7 @@
         else:
             for h in chunks:
                 columns = slice(h * LO, (h + 1) * LO)
-                sens_ref[:, columns] = put_stage(h, put_ref, d_ref) + mid_ref[:, columns]
+                result_ref[64:128, columns] = put_stage(h, put_ref, d_ref) + mid_ref[:, columns]
     total = jnp.zeros((128, x_ref.shape[1]), F32)
     for group in ((0,), (3,), (1,), (2,), (4, 5)):
         parts = []
@@ -380,7 +386,7 @@
         total = total + dot_t(
             jnp.concatenate(parts, 1), list_ref[:, start * LO : (start + 2) * LO]
         )
-    far_ref[...] = total[:64] + total[64:]
+    result_ref[128:192] = total[:64] + total[64:]
     out.wait_send()
     home.wait_send()
 
@@ -392,11 +398,11 @@
 def on_device(density, energy, links, send_index, send_live, face_index):
     blocks = density.shape[1]
     consts = [jnp.asarray(c) for c in constants()]
-    filtered, near, far = pl.pallas_call(
+    result = pl.pallas_call(
         main_kernel,
-        out_shape=[jax.ShapeDtypeStruct((64, blocks), F32)] * 3,
+        out_shape=jax.ShapeDtypeStruct((192, blocks), F32),
         in_specs=[VM] * 4 + [SM] + [VM] * 6,
-        out_specs=[VM] * 3,
+        out_specs=VM,
         scratch_shapes=[
             pltpu.VMEM((26, 1, blocks), jnp.int32),
             pltpu.VMEM((26, 1, blocks), jnp.int32),
@@ -425,6 +431,7 @@
             vmem_limit_bytes=58 * 1024 * 1024, collective_id=0, has_side_effects=True
         ),
     )(density, energy, links, send_index, send_live, face_index, *consts)
+    filtered, near, far = result[:64], result[64:128], result[128:]
     conductivity = FLOOR + filtered * filtered * filtered * (1.0 - FLOOR)
     return conductivity, near + far
 

time: 42.6 us -> 41 us (0.962)
  Pallas kernels: 39.3 us -> 38.3 us
  other arithmetic: 2.48 us -> 1.96 us
    add x1 -> x0, other arithmetic: 1.75 us -> none  [on_device(): conductivity = FLOOR + filtered * filtered * filtered * (1.0 - FLOOR)]
    add x1, other arithmetic: 0.73 us -> 1.96 us  [on_device(): return (conductivity, near + far)]
    pallas_call x1, Pallas kernels: 39.3 us -> 38.3 us  [on_device(): pl.pallas_call(main_kernel, out_shape=jax.ShapeDtypeStruct((192, blocks),...]
where the time goes in v6:
time: 41 us; the launch traced here: 40.9 us
  Pallas kernels  38.3 us (93%)
  other arithmetic  1.96 us (5%)
  between operations  0.64 us (2%)
    pallas_call x1, Pallas kernels, on_device(): pl.pallas_call(main_kernel, out_shape=jax.ShapeDtypeStruct((192, blocks),...  38.3 us
    add x1, other arithmetic, on_device(): return (conductivity, near + far)  1.96 us

profile of v6, /device:TPU:0, one launch (start us, length us, event | category | flops | bytes accessed | tf_op | source)
XLA Modules:
  0.0 40.9 jit_solution(6461026202397304506)
XLA Ops:
  0.6 38.3 %shard_map.122 = f32[192,1024]{1,0:T(8,128)} custom-call(f32[64,1024]{1,0:T(8,128)} %x_ref.1, f32[64,1024]{1,0:T(8,128)} %energy_ref.1, s32[27,1024]{1,0:T(8,128)} %links_ref.1, s32[1,1,4,512]{3,2,1,0:T(4,128)} %index_ref.1, s32[1,1,4]{2,1,0:T(1,128)} %live_ref.1, s32[1,1,2,256]{3,2,1,0:T(2,128)} %face_ref.1, bf16[832,128]{1,0:T(8,128)(2,1)} %constant.14.clone.pick_ref, ...), custom_call_target="tpu_custom_call" | custom-call | tf_op jit(solution)/shard_map/pallas_call | solution.py:401
  38.9 2.0 %slice_add_fusion = (f32[64,1024]{1,0:T(8,128)}, f32[64,1024]{1,0:T(8,128)}) fusion(f32[192,1024]{1,0:T(8,128)} %shard_map.122), kind=kLoop, calls=%fused_computation.3 | loop fusion | flops 327680 | bytes 1310720 | tf_op jit(solution)/shard_map/add | solution.py:436
